TPU v7x, 128 devices: a whole 4x4x4 slice. The times are simulated.
128 devices in a mesh: tile: 16 (over x, z), inf: 8 (over y, core).
Axes of the slice: x: 4, y: 4, z: 4, core: 2. Of those that a mesh axis runs over, the one named last changes fastest.
Arguments:
- u_field: float32 [64, 1024, 1024], P(None, 'tile', 'inf'), may hold values from -6 to 6
- v_field: float32 [64, 1024, 1024], P(None, 'tile', 'inf'), may hold values from -6 to 6
- diffusivity: float32 [1024, 1024], P('tile', 'inf'), may hold values from 0.03 to 0.24
- active_columns: int32 [262144], P(('tile', 'inf')), may hold values from 0 to 8191, as said below
- regimes: int32 [262144, 1], P(('tile', 'inf')), may hold values from 0 to 127; in each aligned block of 2048 rows (0 to 2047, 2048 to 4095, ...) at most 32 rows name the same one
- first_layer: float32 [128, 128, 256], P(('tile', 'inf')), may hold values from -0.5 to 0.5
- second_layer: float32 [128, 256, 256], P(('tile', 'inf')), may hold values from -0.375 to 0.375
- third_layer: float32 [128, 256, 256], P(('tile', 'inf')), may hold values from -0.375 to 0.375
- last_layer: float32 [128, 256, 128], P(('tile', 'inf')), may hold values from -0.375 to 0.375
Outputs:
- u_next: float32 [64, 1024, 1024], P(None, 'tile', 'inf')
- v_next: float32 [64, 1024, 1024], P(None, 'tile', 'inf')
Inputs may be any that keep to these rules, and one draw needn't show every extreme that they name: `active_columns`: the 2048 entries of one device are distinct flat indices x * 128 + y of columns of its own tile. `regimes`: among the rows of one device no network is named more than 32 times.
All inputs are finite; a program needn't handle non-finite values.
Results may differ from a plain program's by a relative error of at most 0.0003.
Values sent between devices are 32-bit elements; how exact they have to be, the bound alone decides.
A program may use at most 128 MiB of HBM per device.

v0:
```python
import jax
import jax.numpy as jnp
from jax import lax
from jax.sharding import PartitionSpec as P

PASSES = 4


def with_halo(x, sides, width):
    for axis, dim in sides:
        count, length = (lax.axis_size(axis), x.shape[dim])
        up = [(i, (i + 1) % count) for i in range(count - 1)]
        down = [(j, i) for i, j in up]
        last = lax.slice_in_dim(x, length - width, length, axis=dim)
        first = lax.slice_in_dim(x, 0, width, axis=dim)
        before = lax.ppermute(last, axis, up)
        after = lax.ppermute(first, axis, down)
        x = jnp.concatenate([before, x, after], axis=dim)
    return x


def standardize(rows):
    center = jnp.mean(rows, axis=-1, keepdims=True)
    spread = jnp.mean(jnp.square(rows - center), axis=-1, keepdims=True)
    return (rows - center) * lax.rsqrt(spread + 1e-05)


def network_rows(rows, first_layer, second_layer, third_layer, last_layer):
    highest = lax.Precision.HIGHEST
    hidden = jax.nn.silu(jnp.dot(rows, first_layer, precision=highest))
    hidden = jax.nn.silu(jnp.dot(hidden, second_layer, precision=highest))
    hidden = jax.nn.silu(jnp.dot(hidden, third_layer, precision=highest))
    return jnp.dot(hidden, last_layer, precision=highest)


def single_pass(padded, center, coeffs):
    neighbours = padded[:, :, 2:, 1:-1] + padded[:, :, :-2, 1:-1]
    neighbours = neighbours + padded[:, :, 1:-1, 2:] + padded[:, :, 1:-1, :-2]
    return center + coeffs * (neighbours - 4.0 * center)


def body(
    u_field,
    v_field,
    diffusivity,
    active_columns,
    regimes,
    first_layer,
    second_layer,
    third_layer,
    last_layer,
):
    levels, width_x, width_y = u_field.shape
    features = 2 * levels
    cells = width_x * width_y
    active_count = active_columns.shape[0]
    devices_all = lax.axis_size(("tile", "inf"))
    capacity = 2 * active_count // devices_all
    slot_total = devices_all * capacity
    block_rows = min(512, active_count)
    block_count = active_count // block_rows
    state = jnp.stack([u_field, v_field])
    target = regimes[:, 0]
    labels = jnp.arange(devices_all, dtype=jnp.int32)
    one_hot = (
        (target[:, None] == labels[None, :])
        .astype(jnp.bfloat16)
        .reshape(block_count, block_rows, devices_all)
    )
    row_ids = jnp.arange(block_rows, dtype=jnp.int32)
    lower = (row_ids[:, None] > row_ids[None, :]).astype(jnp.bfloat16)

    def rank_step(counts, piece):
        earlier = jnp.dot(lower, piece, preferred_element_type=jnp.float32) + counts[None, :]
        wide_piece = piece.astype(jnp.float32)
        rank = jnp.sum(earlier * wide_piece, axis=1)
        return (counts + jnp.sum(wide_piece, axis=0), rank)

    _, ranks = lax.scan(rank_step, jnp.zeros((devices_all,), jnp.float32), one_hot)
    slot_index = target * capacity + ranks.reshape(-1).astype(jnp.int32)
    flat_state = state.reshape(features, cells)
    inputs = flat_state[:, active_columns].T
    outgoing = jnp.zeros((slot_total, features), jnp.float32).at[slot_index].set(inputs)
    block = lax.all_to_all(
        outgoing.reshape(devices_all, capacity, features),
        ("tile", "inf"),
        split_axis=0,
        concat_axis=0,
        tiled=True,
    )
    block_shape = block.shape
    rows = standardize(block.reshape(-1, features))
    result = network_rows(rows, first_layer[0], second_layer[0], third_layer[0], last_layer[0])
    answered = result.reshape(block_shape)
    returned = lax.all_to_all(answered, ("tile", "inf"), split_axis=0, concat_axis=0, tiled=True)
    returned_rows = returned.reshape(slot_total, features)
    drag_rows = returned_rows[slot_index]
    for step_index in range(PASSES):
        padded = with_halo(state, (("tile", 2), ("inf", 3)), 1)
        state = single_pass(padded, state, diffusivity)
    final_flat = state.reshape(features, cells).at[:, active_columns].add(drag_rows.T)
    result = final_flat.reshape(2, levels, width_x, width_y)
    return (result[0], result[1])


def solution(mesh):
    in_specs = (
        P(None, "tile", "inf"),
        P(None, "tile", "inf"),
        P("tile", "inf"),
        P(("tile", "inf")),
        P(("tile", "inf"), None),
        P(("tile", "inf"), None, None),
        P(("tile", "inf"), None, None),
        P(("tile", "inf"), None, None),
        P(("tile", "inf"), None, None),
    )
    out_specs = (P(None, "tile", "inf"), P(None, "tile", "inf"))
    return jax.shard_map(body, mesh=mesh, in_specs=in_specs, out_specs=out_specs, check_vma=False)
```

profile of v0, /device:TPU:3, one launch (start us, length us, event | category | flops | bytes accessed | tf_op | source)
XLA Modules:
  0.0 388.3 jit_solution(2947966674470216051)
XLA Ops:
  19.7 4.8 %fusion.70 = (f32[2,64,66,1]{3,1,2,0:T(8,128)}, f32[2,64,66,1]{3,1,2,0:T(8,128)}) fusion(f32[2,64,66,128]{3,1,2,0:T(8,128)S(1)} %pad_maximum_fusion.1), kind=kLoop, calls=%fused_computation.132 | loop fusion | bytes 135168 | tf_op jit(solution)/shard_map/slice | solution.py:15
  42.2 4.8 %copy.62 = f32[2,64,66,1]{3,1,2,0:T(8,128)} copy(f32[2,64,66,1]{2,1,3,0:T(8,128)S(1)} %collective-permute-done.2) | data formatting | bytes 67584 | tf_op jit(solution)/shard_map/ppermute | solution.py:17
  51.7 12.4 %fusion.31 = f32[2,64,64,128]{3,1,2,0:T(8,128)S(1)} fusion(f32[2,64,66,1]{3,1,2,0:T(8,128)} %copy.64, f32[2,64,1,128]{3,1,2,0:T(8,128)S(1)} %collective-permute-done, f32[2,64,1,128]{3,1,2,0:T(8,128)S(1)} %collective-permute-done.1, f32[1,64,64,128]{3,1,2,0:T(8,128)S(1)} %get-tuple-element.87, f32[1,64,64,128]{3,1,2,0:T(8,128)} %copy-done.2, ...), kind=kLoop, calls=%fused_computation.71 | loop fusion | flops 20971520 | bytes 8620032 | tf_op jit(solution)/shard_map/add | solution.py:39
  66.3 5.3 %collective-permute-start.4 = (f32[2,64,1,128]{3,1,2,0:T(8,128)S(1)}, f32[2,64,1,128]{3,1,2,0:T(8,128)S(1)}, u32[]{:S(2)}, u32[]{:S(2)}) collective-permute-start(f32[2,64,1,128]{3,1,2,0:T(8,128)S(1)} %get-tuple-element.82), channel_id=1, source_target_pairs={{8,0},{16,8},{24,16},{32,24},{40,32},{48,40},{56,48},{64,56},{72,6... | collective-permute-start | bytes 196616 | tf_op jit(solution)/shard_map/ppermute | solution.py:17
  73.5 4.8 %fusion.69 = (f32[2,64,66,1]{3,1,2,0:T(8,128)}, f32[2,64,66,1]{3,1,2,0:T(8,128)}) fusion(f32[2,64,66,128]{3,1,2,0:T(8,128)S(1)} %pad_maximum_fusion.2), kind=kLoop, calls=%fused_computation.131 | loop fusion | bytes 135168 | tf_op jit(solution)/shard_map/slice | solution.py:15
  95.5 10.9 %copy.88 = f32[2,64,64,128]{1,0,3,2:T(2,128)} copy(f32[2,64,64,128]{3,1,2,0:T(8,128)} %pad_maximum_fusion) | data formatting | bytes 8388608 | tf_op jit(solution)/shard_map/reshape | solution.py:81
  106.4 8.8 %reshape.121 = f32[128,8192]{0,1:T(8,128)} reshape(f32[2,64,64,128]{1,0,3,2:T(2,128)} %copy.88) | data formatting | bytes 8388608 | tf_op jit(solution)/shard_map/reshape | solution.py:81
  115.2 18.5 %scatter_custom_fusion = f32[4096,128]{1,0:T(8,128)} fusion(s32[2048]{0:T(1024)S(1)} %bitcast.63, f32[128,8192]{0,1:T(8,128)} %reshape.121, s32[2048]{0:T(1024)S(1)} %get-tuple-element.85, f32[]{:T(128)} %constant.20.clone.1), kind=kCustom, calls=%fused_computation.106 | custom fusion | bytes 2097664 | tf_op jit(solution)/shard_map/scatter | solution.py:83
  133.7 11.4 %all-to-all-start = ((f32[128,32,128]{2,1,0:T(8,128)}), f32[128,32,128]{2,1,0:T(8,128)S(1)}, u32[]{:S(2)}, u32[]{:S(2)}) async-start(f32[128,32,128]{2,1,0:T(8,128)} %bitcast.59), calls=%async_computation | async-start | bytes 4194304 | tf_op jit(solution)/shard_map/all_to_all | solution.py:84
  145.2 4.8 %copy.66 = f32[2,64,66,1]{3,1,2,0:T(8,128)} copy(f32[2,64,66,1]{2,1,3,0:T(8,128)S(1)} %collective-permute-done.6) | data formatting | bytes 67584 | tf_op jit(solution)/shard_map/ppermute | solution.py:17
  154.7 13.7 %fusion.25 = f32[2,64,64,128]{3,1,2,0:T(8,128)S(1)} fusion(f32[2,64,64,128]{3,1,2,0:T(8,128)} %copy-done.3, f32[2,64,66,1]{3,1,2,0:T(8,128)} %copy.68, f32[2,64,1,128]{3,1,2,0:T(8,128)S(1)} %collective-permute-done.4, f32[2,64,1,128]{3,1,2,0:T(8,128)S(1)} %collective-permute-done.5, f32[2,64,66,1]{3,1,2,0:T(8,128)} %copy.66, f32[64,128]{1,0:T(8,128)S(1)} %copy-done.5), kind=kLoop, calls=%fused_computation.57 | loop fusion | flops 15728640 | bytes 8620032 | tf_op jit(solution)/shard_map/add | solution.py:39
  177.8 4.8 %fusion.68 = (f32[2,64,66,1]{3,1,2,0:T(8,128)}, f32[2,64,66,1]{3,1,2,0:T(8,128)}) fusion(f32[2,64,66,128]{3,1,2,0:T(8,128)S(1)} %pad_maximum_fusion.3), kind=kLoop, calls=%fused_computation.130 | loop fusion | bytes 135168 | tf_op jit(solution)/shard_map/slice | solution.py:15
  196.9 4.8 %copy.70 = f32[2,64,66,1]{3,1,2,0:T(8,128)} copy(f32[2,64,66,1]{2,1,3,0:T(8,128)S(1)} %collective-permute-done.10) | data formatting | bytes 67584 | tf_op jit(solution)/shard_map/ppermute | solution.py:17
  206.5 15.7 %fusion.19 = f32[2,64,64,128]{3,1,2,0:T(8,128)} fusion(f32[2,64,64,128]{3,1,2,0:T(8,128)} %copy-done.4, f32[2,64,66,1]{3,1,2,0:T(8,128)} %copy.72, f32[2,64,1,128]{3,1,2,0:T(8,128)S(1)} %collective-permute-done.8, f32[2,64,1,128]{3,1,2,0:T(8,128)S(1)} %collective-permute-done.9, f32[2,64,66,1]{3,1,2,0:T(8,128)} %copy.70, f32[64,128]{1,0:T(8,128)S(1)} %copy-done.5), kind=kLoop, calls=%fused_computation.43 | loop fusion | flops 15728640 | bytes 8620032 | tf_op jit(solution)/shard_map/add | solution.py:39
  237.9 4.7 %fusion.58 = f32[128,32,128]{2,1,0:T(8,128)} fusion(f32[128,32,256]{2,1,0:T(8,128)S(1)} %bitcast.60, f32[1,256,128]{2,1,0:T(8,128)S(1)} %copy-done.7), kind=kOutput, calls=%fused_computation.113 | convolution fusion | flops 1610612736 | bytes 6422528 | tf_op jit(solution)/shard_map/dot_general | solution.py:33
  242.6 10.0 %all-to-all-start.1 = ((f32[128,32,128]{2,1,0:T(8,128)}), f32[128,32,128]{2,1,0:T(8,128)S(1)}, u32[]{:S(2)}, u32[]{:S(2)}) async-start(f32[128,32,128]{2,1,0:T(8,128)} %fusion.58), calls=%async_computation.1 | async-start | bytes 4194304 | tf_op jit(solution)/shard_map/all_to_all | solution.py:95
  260.9 19.8 %collective-permute-done.13 = f32[2,64,1,128]{3,1,2,0:T(8,128)S(1)} collective-permute-done((f32[2,64,1,128]{3,1,2,0:T(8,128)S(1)}, f32[2,64,1,128]{3,1,2,0:T(8,128)S(1)}, u32[]{:S(2)}, u32[]{:S(2)}) %collective-permute-start.13) | collective-permute-done | bytes 65568 | tf_op jit(solution)/shard_map/ppermute | solution.py:16
  283.2 4.8 %fusion.67 = (f32[2,64,66,1]{3,1,2,0:T(8,128)}, f32[2,64,66,1]{3,1,2,0:T(8,128)}) fusion(f32[2,64,66,128]{3,1,2,0:T(8,128)S(1)} %pad_maximum_fusion.4), kind=kLoop, calls=%fused_computation.129 | loop fusion | bytes 135168 | tf_op jit(solution)/shard_map/slice | solution.py:15
  305.6 5.1 %copy.74 = f32[2,64,66,1]{3,1,2,0:T(8,128)} copy(f32[2,64,66,1]{2,1,3,0:T(8,128)S(1)} %collective-permute-done.14) | data formatting | bytes 67584 | tf_op jit(solution)/shard_map/ppermute | solution.py:17
  315.4 15.0 %fusion.13 = f32[2,64,64,128]{3,1,2,0:T(8,128)} fusion(f32[2,64,64,128]{3,1,2,0:T(8,128)} %fusion.19, f32[2,64,66,1]{3,1,2,0:T(8,128)} %copy.76, f32[2,64,1,128]{3,1,2,0:T(8,128)S(1)} %collective-permute-done.12, f32[2,64,1,128]{3,1,2,0:T(8,128)S(1)} %collective-permute-done.13, f32[2,64,66,1]{3,1,2,0:T(8,128)} %copy.74, f32[64,128]{1,0:T(8,128)S(1)} %copy-done.5), kind=kLoop, calls=%fused_computation.29 | loop fusion | flops 15728640 | bytes 8620032 | tf_op jit(solution)/shard_map/add | solution.py:39
  330.4 10.9 %copy.87 = f32[2,64,64,128]{1,0,3,2:T(2,128)} copy(f32[2,64,64,128]{3,1,2,0:T(8,128)} %fusion.13) | data formatting | bytes 8388608 | tf_op jit(solution)/shard_map/reshape | solution.py:101
  341.3 8.8 %reshape.120 = f32[128,8192]{0,1:T(8,128)} reshape(f32[2,64,64,128]{1,0,3,2:T(2,128)} %copy.87) | data formatting | bytes 8388608 | tf_op jit(solution)/shard_map/reshape | solution.py:101
  350.1 21.6 %scatter_custom_fusion.1 = f32[128,8192]{0,1:T(8,128)} fusion(f32[128,8192]{0,1:T(8,128)} %reshape.120, s32[2048]{0:T(1024)S(1)} %get-tuple-element.86, f32[4096,128]{1,0:T(8,128)S(1)} %bitcast.61, s32[2048]{0:T(1024)S(1)} %broadcast_clamp_fusion), kind=kCustom, calls=%fused_computation.104 | custom fusion | flops 262144 | bytes 4194304 | tf_op jit(solution)/shard_map/scatter-add | solution.py:101
  371.6 7.9 %fusion.71 = (f32[64,8192]{0,1:T(8,128)}, f32[64,8192]{0,1:T(8,128)}) fusion(f32[128,8192]{0,1:T(8,128)} %scatter_custom_fusion.1), kind=kLoop, calls=%fused_computation.133 | loop fusion | bytes 8388608 | tf_op jit(solution)/shard_map/slice | solution.py:103
  (114 shorter events, 154.6 us)
Async XLA Ops:
  0.6 228.4 %copy-start = (f32[1,256,256]{2,1,0:T(8,128)S(1)}, f32[1,256,256]{2,1,0:T(8,128)}, u32[]{:S(2)}) copy-start(f32[1,256,256]{2,1,0:T(8,128)} %param.17) | copy-start | bytes 786436
  5.4 9.4 %copy-start.8 = (s32[2048,1]{0,1:T(1,128)S(1)}, s32[2048,1]{0,1:T(1,128)}, u32[]{:S(2)}) copy-start(s32[2048,1]{0,1:T(1,128)} %param.15) | copy-start | bytes 24580
  6.7 11.0 %collective-permute-start.1 = (f32[2,64,1,128]{3,1,2,0:T(8,128)S(1)}, f32[2,64,1,128]{3,1,2,0:T(8,128)S(1)}, u32[]{:S(2)}, u32[]{:S(2)}) collective-permute-start(f32[2,64,1,128]{3,1,2,0:T(8,128)S(1)} %get-tuple-element.83), channel_id=1, source_target_pairs={{0,8},{8,16},{16,24},{24,32},{32,40},{40,48},{48,56},{56,64},{64,7... | collective-permute-start | bytes 196616 | tf_op jit(solution)/shard_map/ppermute | solution.py:16
  10.2 7.5 %collective-permute-start = (f32[2,64,1,128]{3,1,2,0:T(8,128)S(1)}, f32[2,64,1,128]{3,1,2,0:T(8,128)S(1)}, u32[]{:S(2)}, u32[]{:S(2)}) collective-permute-start(f32[2,64,1,128]{3,1,2,0:T(8,128)S(1)} %get-tuple-element.84), channel_id=1, source_target_pairs={{8,0},{16,8},{24,16},{32,24},{40,32},{48,40},{56,48},{64,56},{72,6... | collective-permute-start | bytes 196616 | tf_op jit(solution)/shard_map/ppermute | solution.py:17
  32.5 14.6 %collective-permute-start.3 = (f32[2,64,66,1]{2,1,3,0:T(8,128)S(1)}, f32[2,64,66,1]{2,1,3,0:T(8,128)S(1)}, u32[]{:S(2)}, u32[]{:S(2)}) collective-permute-start(f32[2,64,66,1]{2,1,3,0:T(8,128)S(1)} %copy.63), channel_id=1, source_target_pairs={{0,1},{1,2},{2,3},{3,4},{4,5},{5,6},{6,7},{8,9},{9,10},{10,11},{11... | collective-permute-start | bytes 101384 | tf_op jit(solution)/shard_map/ppermute | solution.py:16
  36.6 5.6 %collective-permute-start.2 = (f32[2,64,66,1]{2,1,3,0:T(8,128)S(1)}, f32[2,64,66,1]{2,1,3,0:T(8,128)S(1)}, u32[]{:S(2)}, u32[]{:S(2)}) collective-permute-start(f32[2,64,66,1]{2,1,3,0:T(8,128)S(1)} %copy.61), channel_id=1, source_target_pairs={{1,0},{2,1},{3,2},{4,3},{5,4},{6,5},{7,6},{9,8},{10,9},{11,10},{12... | collective-permute-start | bytes 101384 | tf_op jit(solution)/shard_map/ppermute | solution.py:17
  38.7 13.0 %copy-start.5 = (f32[64,128]{1,0:T(8,128)S(1)}, f32[64,128]{1,0:T(8,128)}, u32[]{:S(2)}) copy-start(f32[64,128]{1,0:T(8,128)} %param.13) | copy-start | bytes 98308
  51.7 19.8 %copy-start.9 = (s32[2048]{0:T(1024)S(1)}, s32[2048]{0:T(1024)}, u32[]{:S(2)}) copy-start(s32[2048]{0:T(1024)} %param.14) | copy-start | bytes 24580
  64.1 9.4 %copy-start.3 = (f32[2,64,64,128]{3,1,2,0:T(8,128)}, f32[2,64,64,128]{3,1,2,0:T(8,128)S(1)}, u32[]{:S(2)}) copy-start(f32[2,64,64,128]{3,1,2,0:T(8,128)S(1)} %fusion.31) | copy-start | bytes 12582916
  64.2 7.4 %collective-permute-start.5 = (f32[2,64,1,128]{3,1,2,0:T(8,128)S(1)}, f32[2,64,1,128]{3,1,2,0:T(8,128)S(1)}, u32[]{:S(2)}, u32[]{:S(2)}) collective-permute-start(f32[2,64,1,128]{3,1,2,0:T(8,128)S(1)} %get-tuple-element.81), channel_id=1, source_target_pairs={{0,8},{8,16},{16,24},{24,32},{32,40},{40,48},{48,56},{56,64},{64,7... | collective-permute-start | bytes 196616 | tf_op jit(solution)/shard_map/ppermute | solution.py:16
  66.3 6.6 %collective-permute-start.4 = (f32[2,64,1,128]{3,1,2,0:T(8,128)S(1)}, f32[2,64,1,128]{3,1,2,0:T(8,128)S(1)}, u32[]{:S(2)}, u32[]{:S(2)}) collective-permute-start(f32[2,64,1,128]{3,1,2,0:T(8,128)S(1)} %get-tuple-element.82), channel_id=1, source_target_pairs={{8,0},{16,8},{24,16},{32,24},{40,32},{48,40},{56,48},{64,56},{72,6... | collective-permute-start | bytes 196616 | tf_op jit(solution)/shard_map/ppermute | solution.py:17
  86.2 63.8 %collective-permute-start.7 = (f32[2,64,66,1]{2,1,3,0:T(8,128)S(1)}, f32[2,64,66,1]{2,1,3,0:T(8,128)S(1)}, u32[]{:S(2)}, u32[]{:S(2)}) collective-permute-start(f32[2,64,66,1]{2,1,3,0:T(8,128)S(1)} %copy.67), channel_id=1, source_target_pairs={{0,1},{1,2},{2,3},{3,4},{4,5},{5,6},{6,7},{8,9},{9,10},{10,11},{11... | collective-permute-start | bytes 101384 | tf_op jit(solution)/shard_map/ppermute | solution.py:16
  89.4 55.8 %collective-permute-start.6 = (f32[2,64,66,1]{2,1,3,0:T(8,128)S(1)}, f32[2,64,66,1]{2,1,3,0:T(8,128)S(1)}, u32[]{:S(2)}, u32[]{:S(2)}) collective-permute-start(f32[2,64,66,1]{2,1,3,0:T(8,128)S(1)} %copy.65), channel_id=1, source_target_pairs={{1,0},{2,1},{3,2},{4,3},{5,4},{6,5},{7,6},{9,8},{10,9},{11,10},{12... | collective-permute-start | bytes 101384 | tf_op jit(solution)/shard_map/ppermute | solution.py:17
  133.7 88.5 %all-to-all-start = ((f32[128,32,128]{2,1,0:T(8,128)}), f32[128,32,128]{2,1,0:T(8,128)S(1)}, u32[]{:S(2)}, u32[]{:S(2)}) async-start(f32[128,32,128]{2,1,0:T(8,128)} %bitcast.59), calls=%async_computation | async-start | bytes 4194304 | tf_op jit(solution)/shard_map/all_to_all | solution.py:84
  168.4 9.4 %copy-start.4 = (f32[2,64,64,128]{3,1,2,0:T(8,128)}, f32[2,64,64,128]{3,1,2,0:T(8,128)S(1)}, u32[]{:S(2)}) copy-start(f32[2,64,64,128]{3,1,2,0:T(8,128)S(1)} %fusion.25) | copy-start | bytes 12582916
  168.4 7.8 %collective-permute-start.9 = (f32[2,64,1,128]{3,1,2,0:T(8,128)S(1)}, f32[2,64,1,128]{3,1,2,0:T(8,128)S(1)}, u32[]{:S(2)}, u32[]{:S(2)}) collective-permute-start(f32[2,64,1,128]{3,1,2,0:T(8,128)S(1)} %get-tuple-element.79), channel_id=1, source_target_pairs={{0,8},{8,16},{16,24},{24,32},{32,40},{40,48},{48,56},{56,64},{64,7... | collective-permute-start | bytes 196616 | tf_op jit(solution)/shard_map/ppermute | solution.py:16
  171.7 5.5 %collective-permute-start.8 = (f32[2,64,1,128]{3,1,2,0:T(8,128)S(1)}, f32[2,64,1,128]{3,1,2,0:T(8,128)S(1)}, u32[]{:S(2)}, u32[]{:S(2)}) collective-permute-start(f32[2,64,1,128]{3,1,2,0:T(8,128)S(1)} %get-tuple-element.80), channel_id=1, source_target_pairs={{8,0},{16,8},{24,16},{32,24},{40,32},{48,40},{56,48},{64,56},{72,6... | collective-permute-start | bytes 196616 | tf_op jit(solution)/shard_map/ppermute | solution.py:17
  186.5 10.4 %collective-permute-start.10 = (f32[2,64,66,1]{2,1,3,0:T(8,128)S(1)}, f32[2,64,66,1]{2,1,3,0:T(8,128)S(1)}, u32[]{:S(2)}, u32[]{:S(2)}) collective-permute-start(f32[2,64,66,1]{2,1,3,0:T(8,128)S(1)} %copy.69), channel_id=1, source_target_pairs={{1,0},{2,1},{3,2},{4,3},{5,4},{6,5},{7,6},{9,8},{10,9},{11,10},{12... | collective-permute-start | bytes 101384 | tf_op jit(solution)/shard_map/ppermute | solution.py:17
  193.9 7.8 %collective-permute-start.11 = (f32[2,64,66,1]{2,1,3,0:T(8,128)S(1)}, f32[2,64,66,1]{2,1,3,0:T(8,128)S(1)}, u32[]{:S(2)}, u32[]{:S(2)}) collective-permute-start(f32[2,64,66,1]{2,1,3,0:T(8,128)S(1)} %copy.71), channel_id=1, source_target_pairs={{0,1},{1,2},{2,3},{3,4},{4,5},{5,6},{6,7},{8,9},{9,10},{10,11},{11... | collective-permute-start | bytes 101384 | tf_op jit(solution)/shard_map/ppermute | solution.py:16
  242.6 107.5 %all-to-all-start.1 = ((f32[128,32,128]{2,1,0:T(8,128)}), f32[128,32,128]{2,1,0:T(8,128)S(1)}, u32[]{:S(2)}, u32[]{:S(2)}) async-start(f32[128,32,128]{2,1,0:T(8,128)} %fusion.58), calls=%async_computation.1 | async-start | bytes 4194304 | tf_op jit(solution)/shard_map/all_to_all | solution.py:95
  253.5 27.2 %collective-permute-start.13 = (f32[2,64,1,128]{3,1,2,0:T(8,128)S(1)}, f32[2,64,1,128]{3,1,2,0:T(8,128)S(1)}, u32[]{:S(2)}, u32[]{:S(2)}) collective-permute-start(f32[2,64,1,128]{3,1,2,0:T(8,128)S(1)} %get-tuple-element.77), channel_id=1, source_target_pairs={{0,8},{8,16},{16,24},{24,32},{32,40},{40,48},{48,56},{56,64},{64,7... | collective-permute-start | bytes 196616 | tf_op jit(solution)/shard_map/ppermute | solution.py:16
  256.7 24.0 %collective-permute-start.12 = (f32[2,64,1,128]{3,1,2,0:T(8,128)S(1)}, f32[2,64,1,128]{3,1,2,0:T(8,128)S(1)}, u32[]{:S(2)}, u32[]{:S(2)}) collective-permute-start(f32[2,64,1,128]{3,1,2,0:T(8,128)S(1)} %get-tuple-element.78), channel_id=1, source_target_pairs={{8,0},{16,8},{24,16},{32,24},{40,32},{48,40},{56,48},{64,56},{72,6... | collective-permute-start | bytes 196616 | tf_op jit(solution)/shard_map/ppermute | solution.py:17
  295.9 14.7 %collective-permute-start.15 = (f32[2,64,66,1]{2,1,3,0:T(8,128)S(1)}, f32[2,64,66,1]{2,1,3,0:T(8,128)S(1)}, u32[]{:S(2)}, u32[]{:S(2)}) collective-permute-start(f32[2,64,66,1]{2,1,3,0:T(8,128)S(1)} %copy.75), channel_id=1, source_target_pairs={{0,1},{1,2},{2,3},{3,4},{4,5},{5,6},{6,7},{8,9},{9,10},{10,11},{11... | collective-permute-start | bytes 101384 | tf_op jit(solution)/shard_map/ppermute | solution.py:16
  300.0 5.6 %collective-permute-start.14 = (f32[2,64,66,1]{2,1,3,0:T(8,128)S(1)}, f32[2,64,66,1]{2,1,3,0:T(8,128)S(1)}, u32[]{:S(2)}, u32[]{:S(2)}) collective-permute-start(f32[2,64,66,1]{2,1,3,0:T(8,128)S(1)} %copy.73), channel_id=1, source_target_pairs={{1,0},{2,1},{3,2},{4,3},{5,4},{6,5},{7,6},{9,8},{10,9},{11,10},{12... | collective-permute-start | bytes 101384 | tf_op jit(solution)/shard_map/ppermute | solution.py:17
  (5 other events, 21.8 us)
where the time goes:
time: 396 us; the launch traced here: 388 us
  local copies, waits for them, and re-layouts  171 us (43%)
  other arithmetic  92.6 us (23%)
  starting transfers between devices  75.4 us (19%)
  waiting for transfers between devices  29.1 us (7%)
  matrix products  18.2 us (5%)
    add x4, other arithmetic, single_pass(): return center + coeffs * (neighbours - 4.0 * center)  56.7 us
    slice x8, local copies, waits for them, and re-layouts, with_halo(): first = lax.slice_in_dim(x, 0, width, axis=dim)  35 us
    ppermute x8, starting transfers between devices, with_halo(): after = lax.ppermute(first, axis, down)  27.6 us
    ppermute x8, starting transfers between devices, with_halo(): before = lax.ppermute(last, axis, up)  26.5 us
    scatter-add x1, other arithmetic, body(): state.reshape(features, cells).at[:, active_columns].add(drag_rows.T)  21.6 us
    ppermute x8, waiting for transfers between devices, with_halo(): before = lax.ppermute(last, axis, up)  19.8 us
    reshape x2, local copies, waits for them, and re-layouts, body(): flat_state = state.reshape(features, cells)  19.7 us
    reshape x2, local copies, waits for them, and re-layouts, body(): state.reshape(features, cells).at[:, active_columns].add(drag_rows.T)  19.7 us
  transfers between devices with their start and end apart: 18, of which 5 were waited for; matrix products, arithmetic and copies ran while one was open for 44% of the time, Pallas kernels for 0%

commit v1 on v0

--- a/solution.py
+++ b/solution.py
@@ -1,9 +1,78 @@
+import functools
+
 import jax
 import jax.numpy as jnp
 from jax import lax
+from jax.experimental import pallas as pl
+from jax.experimental.pallas import tpu as pltpu
 from jax.sharding import PartitionSpec as P
 
 PASSES = 4
+
+
+def exchange_kernel(count, me_axes, x_ref, o_ref, send_sem, recv_sem, own_sem):
+    me = lax.axis_index("tile") * lax.axis_size("inf") + lax.axis_index("inf")
+
+    def peer(step):
+        return (me + step) % count
+
+    barrier = pltpu.get_barrier_semaphore()
+
+    def greet(step, carry):
+        pl.semaphore_signal(barrier, inc=1, device_id=peer(step), device_id_type=pl.DeviceIdType.LOGICAL)
+        return carry
+
+    lax.fori_loop(1, count, greet, 0)
+    own = pltpu.make_async_copy(x_ref.at[me], o_ref.at[me], own_sem)
+    own.start()
+    pl.semaphore_wait(barrier, count - 1)
+
+    def send(step, carry):
+        other = peer(step)
+        pltpu.make_async_remote_copy(
+            src_ref=x_ref.at[other],
+            dst_ref=o_ref.at[me],
+            send_sem=send_sem.at[step],
+            recv_sem=recv_sem.at[step],
+            device_id=other,
+            device_id_type=pl.DeviceIdType.LOGICAL,
+        ).start()
+        return carry
+
+    lax.fori_loop(1, count, send, 0)
+
+    def finish(step, carry):
+        source = (me - step + count) % count
+        pltpu.make_async_remote_copy(
+            src_ref=x_ref.at[peer(step)],
+            dst_ref=o_ref.at[source],
+            send_sem=send_sem.at[step],
+            recv_sem=recv_sem.at[step],
+            device_id=peer(step),
+            device_id_type=pl.DeviceIdType.LOGICAL,
+        ).wait()
+        return carry
+
+    lax.fori_loop(1, count, finish, 0)
+    own.wait()
+
+
+def exchange(x, number):
+    count = x.shape[0]
+    return pl.pallas_call(
+        functools.partial(exchange_kernel, count, None),
+        out_shape=jax.ShapeDtypeStruct(x.shape, x.dtype),
+        in_specs=[pl.BlockSpec(memory_space=pltpu.VMEM)],
+        out_specs=pl.BlockSpec(memory_space=pltpu.VMEM),
+        scratch_shapes=[
+            pltpu.SemaphoreType.DMA((count,)),
+            pltpu.SemaphoreType.DMA((count,)),
+            pltpu.SemaphoreType.DMA,
+        ],
+        compiler_params=pltpu.CompilerParams(
+            collective_id=number, has_side_effects=True, vmem_limit_bytes=40 << 20
+        ),
+    )(x)
 
 
 def with_halo(x, sides, width):
@@ -81,18 +150,12 @@
     flat_state = state.reshape(features, cells)
     inputs = flat_state[:, active_columns].T
     outgoing = jnp.zeros((slot_total, features), jnp.float32).at[slot_index].set(inputs)
-    block = lax.all_to_all(
-        outgoing.reshape(devices_all, capacity, features),
-        ("tile", "inf"),
-        split_axis=0,
-        concat_axis=0,
-        tiled=True,
-    )
+    block = exchange(outgoing.reshape(devices_all, capacity, features), 0)
     block_shape = block.shape
     rows = standardize(block.reshape(-1, features))
     result = network_rows(rows, first_layer[0], second_layer[0], third_layer[0], last_layer[0])
     answered = result.reshape(block_shape)
-    returned = lax.all_to_all(answered, ("tile", "inf"), split_axis=0, concat_axis=0, tiled=True)
+    returned = exchange(answered, 1)
     returned_rows = returned.reshape(slot_total, features)
     drag_rows = returned_rows[slot_index]
     for step_index in range(PASSES):

time: 396 us -> 448 us (1.13)
  the two profiles are of different devices: /device:TPU:3 before, /device:TPU:121 now
where the time goes in v1:
time: 448 us; the launch traced here: 440 us
  local copies, waits for them, and re-layouts  174 us (39%)
  other arithmetic  96.2 us (21%)
  Pallas kernels  93.1 us (21%)
  starting transfers between devices  49.3 us (11%)
  matrix products  23.3 us (5%)
    pallas_call x2, Pallas kernels, exchange(): pl.pallas_call(functools.partial(exchange_kernel, count, None), out_shape...  93.1 us
    add x4, other arithmetic, single_pass(): return center + coeffs * (neighbours - 4.0 * center)  55.3 us
    slice x8, local copies, waits for them, and re-layouts, with_halo(): first = lax.slice_in_dim(x, 0, width, axis=dim)  35.3 us
    ppermute x8, starting transfers between devices, with_halo(): after = lax.ppermute(first, axis, down)  33 us
    scatter-add x1, other arithmetic, body(): state.reshape(features, cells).at[:, active_columns].add(drag_rows.T)  26.5 us
    reshape x2, local copies, waits for them, and re-layouts, body(): flat_state = state.reshape(features, cells)  19.7 us
    reshape x2, local copies, waits for them, and re-layouts, body(): state.reshape(features, cells).at[:, active_columns].add(drag_rows.T)  19.7 us
    ppermute x4, local copies, waits for them, and re-layouts, with_halo(): after = lax.ppermute(first, axis, down)  19.2 us
  transfers between devices with their start and end apart: 16, of which 3 were waited for; matrix products, arithmetic and copies ran while one was open for 21% of the time, Pallas kernels for 21%

profile of v1, /device:TPU:121, one launch (start us, length us, event | category | flops | bytes accessed | tf_op | source)
XLA Modules:
  0.0 439.9 jit_solution(7886660622865009255)
XLA Ops:
  19.6 10.9 %copy.63 = f32[2,64,64,128]{1,0,3,2:T(2,128)} copy(f32[2,64,64,128]{3,1,2,0:T(8,128)} %pad_maximum_fusion) | data formatting | bytes 8388608 | tf_op jit(solution)/shard_map/reshape | solution.py:150
  30.5 8.8 %reshape.121 = f32[128,8192]{0,1:T(8,128)} reshape(f32[2,64,64,128]{1,0,3,2:T(2,128)} %copy.63) | data formatting | bytes 8388608 | tf_op jit(solution)/shard_map/reshape | solution.py:150
  39.4 18.8 %scatter_custom_fusion = f32[4096,128]{1,0:T(8,128)} fusion(s32[2048]{0:T(1024)S(1)} %bitcast.63, f32[128,8192]{0,1:T(8,128)} %reshape.121, s32[2048]{0:T(1024)S(1)} %get-tuple-element.83, f32[]{:T(128)} %constant.20.clone.1), kind=kCustom, calls=%fused_computation.106 | custom fusion | bytes 2097664 | tf_op jit(solution)/shard_map/scatter | solution.py:152
  59.7 44.7 %shard_map.104 = f32[128,32,128]{2,1,0:T(8,128)S(1)} custom-call(f32[128,32,128]{2,1,0:T(8,128)S(1)} %bitcast.56), custom_call_target="tpu_custom_call" | custom-call | tf_op jit(solution)/shard_map/pallas_call | solution.py:62
  136.5 13.3 %fusion.31 = f32[2,64,64,128]{3,1,2,0:T(8,128)S(1)} fusion(f32[2,64,66,1]{3,1,2,0:T(8,128)} %copy.39, f32[2,64,1,128]{3,1,2,0:T(8,128)S(1)} %collective-permute-done, f32[2,64,1,128]{3,1,2,0:T(8,128)S(1)} %collective-permute-done.1, f32[1,64,64,128]{3,1,2,0:T(8,128)} %copy-done.4, f32[1,64,64,128]{3,1,2,0:T(8,128)} %copy-done.5, f32[2,64,66,1]{3,1,2,0:T(8,128)} %copy.37, ...), kind=kLoop, calls=%fused_computation.71 | loop fusion | flops 20971520 | bytes 8620032 | tf_op jit(solution)/shard_map/add | solution.py:108
  159.5 4.8 %fusion.69 = (f32[2,64,66,1]{3,1,2,0:T(8,128)}, f32[2,64,66,1]{3,1,2,0:T(8,128)}) fusion(f32[2,64,66,128]{3,1,2,0:T(8,128)S(1)} %pad_maximum_fusion.2), kind=kLoop, calls=%fused_computation.131 | loop fusion | bytes 135168 | tf_op jit(solution)/shard_map/slice | solution.py:84
  173.7 6.5 %collective-permute-start.6 = (f32[2,64,66,1]{2,1,3,0:T(8,128)S(1)}, f32[2,64,66,1]{2,1,3,0:T(8,128)S(1)}, u32[]{:S(2)}, u32[]{:S(2)}) collective-permute-start(f32[2,64,66,1]{2,1,3,0:T(8,128)S(1)} %copy.40), channel_id=1, source_target_pairs={{1,0},{2,1},{3,2},{4,3},{5,4},{6,5},{7,6},{9,8},{10,9},{11,10},{12... | collective-permute-start | bytes 101384 | tf_op jit(solution)/shard_map/ppermute | solution.py:86
  180.2 4.9 %fusion.60 = f32[4096,256]{1,0:T(8,128)} fusion(f32[4096,128]{1,0:T(8,128)S(1)} %bitcast.60, f32[1,128,256]{2,1,0:T(8,128)S(1)} %copy-done.13), kind=kOutput, calls=%fused_computation.115 | convolution fusion | flops 1610612736 | bytes 6422528 | tf_op jit(solution)/shard_map/dot_general | solution.py:99
  185.1 4.8 %copy.41 = f32[2,64,66,1]{3,1,2,0:T(8,128)} copy(f32[2,64,66,1]{2,1,3,0:T(8,128)S(1)} %collective-permute-done.6) | data formatting | bytes 67584 | tf_op jit(solution)/shard_map/ppermute | solution.py:86
  194.7 13.6 %fusion.25 = f32[2,64,64,128]{3,1,2,0:T(8,128)S(1)} fusion(f32[2,64,64,128]{3,1,2,0:T(8,128)} %copy-done.6, f32[2,64,66,1]{3,1,2,0:T(8,128)} %copy.43, f32[2,64,1,128]{3,1,2,0:T(8,128)S(1)} %collective-permute-done.4, f32[2,64,1,128]{3,1,2,0:T(8,128)S(1)} %collective-permute-done.5, f32[2,64,66,1]{3,1,2,0:T(8,128)} %copy.41, f32[64,128]{1,0:T(8,128)S(1)} %copy-done.12), kind=kLoop, calls=%fused_computation.57 | loop fusion | flops 15728640 | bytes 8620032 | tf_op jit(solution)/shard_map/add | solution.py:108
  213.8 5.5 %fusion.40 = f32[4096,256]{1,0:T(8,128)} fusion(f32[4096,256]{1,0:T(8,128)S(1)} %copy-done.10, f32[1,256,256]{2,1,0:T(8,128)S(1)} %copy-done), kind=kOutput, calls=%fused_computation.92 | convolution fusion | flops 3225419776 | bytes 8650752 | tf_op jit(solution)/shard_map/dot_general | solution.py:100
  219.9 4.8 %fusion.68 = (f32[2,64,66,1]{3,1,2,0:T(8,128)}, f32[2,64,66,1]{3,1,2,0:T(8,128)}) fusion(f32[2,64,66,128]{3,1,2,0:T(8,128)S(1)} %pad_maximum_fusion.3), kind=kLoop, calls=%fused_computation.130 | loop fusion | bytes 135168 | tf_op jit(solution)/shard_map/slice | solution.py:84
  233.9 5.0 %collective-permute-start.10 = (f32[2,64,66,1]{2,1,3,0:T(8,128)S(1)}, f32[2,64,66,1]{2,1,3,0:T(8,128)S(1)}, u32[]{:S(2)}, u32[]{:S(2)}) collective-permute-start(f32[2,64,66,1]{2,1,3,0:T(8,128)S(1)} %copy.44), channel_id=1, source_target_pairs={{1,0},{2,1},{3,2},{4,3},{5,4},{6,5},{7,6},{9,8},{10,9},{11,10},{12... | collective-permute-start | bytes 101384 | tf_op jit(solution)/shard_map/ppermute | solution.py:86
  239.0 8.3 %divide_multiply_fusion = f32[4096,256]{1,0:T(8,128)} fusion(f32[4096,256]{1,0:T(8,128)} %fusion.40, f32[1,256,256]{2,1,0:T(8,128)S(1)} %copy-done.17), kind=kOutput, calls=%fused_computation.85 | convolution fusion | flops 3229614080 | bytes 8650752 | tf_op jit(solution)/shard_map/dot_general | solution.py:101
  247.3 4.8 %copy.45 = f32[2,64,66,1]{3,1,2,0:T(8,128)} copy(f32[2,64,66,1]{2,1,3,0:T(8,128)S(1)} %collective-permute-done.10) | data formatting | bytes 67584 | tf_op jit(solution)/shard_map/ppermute | solution.py:86
  256.8 13.6 %fusion.19 = f32[2,64,64,128]{3,1,2,0:T(8,128)S(1)} fusion(f32[2,64,64,128]{3,1,2,0:T(8,128)} %copy-done.8, f32[2,64,66,1]{3,1,2,0:T(8,128)} %copy.47, f32[2,64,1,128]{3,1,2,0:T(8,128)S(1)} %collective-permute-done.8, f32[2,64,1,128]{3,1,2,0:T(8,128)S(1)} %collective-permute-done.9, f32[2,64,66,1]{3,1,2,0:T(8,128)} %copy.45, f32[64,128]{1,0:T(8,128)S(1)} %copy-done.12), kind=kLoop, calls=%fused_computation.43 | loop fusion | flops 15728640 | bytes 8620032 | tf_op jit(solution)/shard_map/add | solution.py:108
  296.9 6.2 %collective-permute-start.14 = (f32[2,64,66,1]{2,1,3,0:T(8,128)S(1)}, f32[2,64,66,1]{2,1,3,0:T(8,128)S(1)}, u32[]{:S(2)}, u32[]{:S(2)}) collective-permute-start(f32[2,64,66,1]{2,1,3,0:T(8,128)S(1)} %copy.48), channel_id=1, source_target_pairs={{1,0},{2,1},{3,2},{4,3},{5,4},{6,5},{7,6},{9,8},{10,9},{11,10},{12... | collective-permute-start | bytes 101384 | tf_op jit(solution)/shard_map/ppermute | solution.py:86
  303.1 48.3 %shard_map.105 = f32[128,32,128]{2,1,0:T(8,128)S(1)} custom-call(f32[128,32,128]{2,1,0:T(8,128)S(1)} %fusion.58.x_ref), custom_call_target="tpu_custom_call" | custom-call | tf_op jit(solution)/shard_map/pallas_call | solution.py:62
  352.8 4.8 %copy.49 = f32[2,64,66,1]{3,1,2,0:T(8,128)} copy(f32[2,64,66,1]{2,1,3,0:T(8,128)S(1)} %collective-permute-done.14) | data formatting | bytes 67584 | tf_op jit(solution)/shard_map/ppermute | solution.py:86
  362.3 14.9 %fusion.13 = f32[2,64,64,128]{3,1,2,0:T(8,128)} fusion(f32[2,64,64,128]{3,1,2,0:T(8,128)} %copy-done.7, f32[2,64,66,1]{3,1,2,0:T(8,128)} %copy.51, f32[2,64,1,128]{3,1,2,0:T(8,128)S(1)} %collective-permute-done.12, f32[2,64,1,128]{3,1,2,0:T(8,128)S(1)} %collective-permute-done.13, f32[2,64,66,1]{3,1,2,0:T(8,128)} %copy.49, f32[64,128]{1,0:T(8,128)S(1)} %copy-done.12), kind=kLoop, calls=%fused_computation.29 | loop fusion | flops 15728640 | bytes 8620032 | tf_op jit(solution)/shard_map/add | solution.py:108
  377.2 10.9 %copy.62 = f32[2,64,64,128]{1,0,3,2:T(2,128)} copy(f32[2,64,64,128]{3,1,2,0:T(8,128)} %fusion.13) | data formatting | bytes 8388608 | tf_op jit(solution)/shard_map/reshape | solution.py:164
  388.1 8.8 %reshape.120 = f32[128,8192]{0,1:T(8,128)} reshape(f32[2,64,64,128]{1,0,3,2:T(2,128)} %copy.62) | data formatting | bytes 8388608 | tf_op jit(solution)/shard_map/reshape | solution.py:164
  396.9 26.5 %scatter_custom_fusion.1 = f32[128,8192]{0,1:T(8,128)} fusion(f32[128,8192]{0,1:T(8,128)} %reshape.120, s32[2048]{0:T(1024)S(1)} %get-tuple-element.84, f32[4096,128]{1,0:T(8,128)} %bitcast.57, s32[2048]{0:T(1024)S(1)} %broadcast_clamp_fusion), kind=kCustom, calls=%fused_computation.104 | custom fusion | flops 262144 | bytes 4194304 | tf_op jit(solution)/shard_map/scatter-add | solution.py:164
  423.4 7.9 %fusion.71 = (f32[64,8192]{0,1:T(8,128)}, f32[64,8192]{0,1:T(8,128)}) fusion(f32[128,8192]{0,1:T(8,128)} %scatter_custom_fusion.1), kind=kLoop, calls=%fused_computation.133 | loop fusion | bytes 8388608 | tf_op jit(solution)/shard_map/slice | solution.py:166
  (126 shorter events, 139.0 us)
Async XLA Ops:
  0.6 213.1 %copy-start = (f32[1,256,256]{2,1,0:T(8,128)S(1)}, f32[1,256,256]{2,1,0:T(8,128)}, u32[]{:S(2)}) copy-start(f32[1,256,256]{2,1,0:T(8,128)} %param.17) | copy-start | bytes 786436
  6.7 99.7 %collective-permute-start.1 = (f32[2,64,1,128]{3,1,2,0:T(8,128)S(1)}, f32[2,64,1,128]{3,1,2,0:T(8,128)S(1)}, u32[]{:S(2)}, u32[]{:S(2)}) collective-permute-start(f32[2,64,1,128]{3,1,2,0:T(8,128)S(1)} %get-tuple-element.81), channel_id=1, source_target_pairs={{0,8},{8,16},{16,24},{24,32},{32,40},{40,48},{48,56},{56,64},{64,7... | collective-permute-start | bytes 196616 | tf_op jit(solution)/shard_map/ppermute | solution.py:85
  8.6 97.8 %collective-permute-start = (f32[2,64,1,128]{3,1,2,0:T(8,128)S(1)}, f32[2,64,1,128]{3,1,2,0:T(8,128)S(1)}, u32[]{:S(2)}, u32[]{:S(2)}) collective-permute-start(f32[2,64,1,128]{3,1,2,0:T(8,128)S(1)} %get-tuple-element.82), channel_id=1, source_target_pairs={{8,0},{16,8},{24,16},{32,24},{40,32},{48,40},{56,48},{64,56},{72,6... | collective-permute-start | bytes 196616 | tf_op jit(solution)/shard_map/ppermute | solution.py:86
  121.7 10.0 %collective-permute-start.3 = (f32[2,64,66,1]{2,1,3,0:T(8,128)S(1)}, f32[2,64,66,1]{2,1,3,0:T(8,128)S(1)}, u32[]{:S(2)}, u32[]{:S(2)}) collective-permute-start(f32[2,64,66,1]{2,1,3,0:T(8,128)S(1)} %copy.38), channel_id=1, source_target_pairs={{0,1},{1,2},{2,3},{3,4},{4,5},{5,6},{6,7},{8,9},{9,10},{10,11},{11... | collective-permute-start | bytes 101384 | tf_op jit(solution)/shard_map/ppermute | solution.py:85
  123.0 3.9 collective-permute-start.2
  149.8 8.5 %collective-permute-start.5 = (f32[2,64,1,128]{3,1,2,0:T(8,128)S(1)}, f32[2,64,1,128]{3,1,2,0:T(8,128)S(1)}, u32[]{:S(2)}, u32[]{:S(2)}) collective-permute-start(f32[2,64,1,128]{3,1,2,0:T(8,128)S(1)} %get-tuple-element.79), channel_id=1, source_target_pairs={{0,8},{8,16},{16,24},{24,32},{32,40},{40,48},{48,56},{56,64},{64,7... | collective-permute-start | bytes 196616 | tf_op jit(solution)/shard_map/ppermute | solution.py:85
  151.8 7.1 %collective-permute-start.4 = (f32[2,64,1,128]{3,1,2,0:T(8,128)S(1)}, f32[2,64,1,128]{3,1,2,0:T(8,128)S(1)}, u32[]{:S(2)}, u32[]{:S(2)}) collective-permute-start(f32[2,64,1,128]{3,1,2,0:T(8,128)S(1)} %get-tuple-element.80), channel_id=1, source_target_pairs={{8,0},{16,8},{24,16},{32,24},{40,32},{48,40},{56,48},{64,56},{72,6... | collective-permute-start | bytes 196616 | tf_op jit(solution)/shard_map/ppermute | solution.py:86
  164.3 15.9 %copy-start.9 = (f32[128,32,128]{2,1,0:T(8,128)S(1)}, f32[128,32,128]{2,1,0:T(8,128)}, u32[]{:S(2)}) copy-start(f32[128,32,128]{2,1,0:T(8,128)} %subtract_multiply_fusion) | copy-start | bytes 6291460
  164.3 15.9 %copy-start.13 = (f32[1,128,256]{2,1,0:T(8,128)S(1)}, f32[1,128,256]{2,1,0:T(8,128)}, u32[]{:S(2)}) copy-start(f32[1,128,256]{2,1,0:T(8,128)} %param.16) | copy-start | bytes 393220
  172.4 17.5 %collective-permute-start.7 = (f32[2,64,66,1]{2,1,3,0:T(8,128)S(1)}, f32[2,64,66,1]{2,1,3,0:T(8,128)S(1)}, u32[]{:S(2)}, u32[]{:S(2)}) collective-permute-start(f32[2,64,66,1]{2,1,3,0:T(8,128)S(1)} %copy.42), channel_id=1, source_target_pairs={{0,1},{1,2},{2,3},{3,4},{4,5},{5,6},{6,7},{8,9},{9,10},{10,11},{11... | collective-permute-start | bytes 101384 | tf_op jit(solution)/shard_map/ppermute | solution.py:85
  173.7 11.4 %collective-permute-start.6 = (f32[2,64,66,1]{2,1,3,0:T(8,128)S(1)}, f32[2,64,66,1]{2,1,3,0:T(8,128)S(1)}, u32[]{:S(2)}, u32[]{:S(2)}) collective-permute-start(f32[2,64,66,1]{2,1,3,0:T(8,128)S(1)} %copy.40), channel_id=1, source_target_pairs={{1,0},{2,1},{3,2},{4,3},{5,4},{6,5},{7,6},{9,8},{10,9},{11,10},{12... | collective-permute-start | bytes 101384 | tf_op jit(solution)/shard_map/ppermute | solution.py:86
  194.7 19.1 %copy-start.10 = (f32[4096,256]{1,0:T(8,128)S(1)}, f32[4096,256]{1,0:T(8,128)}, u32[]{:S(2)}) copy-start(f32[4096,256]{1,0:T(8,128)} %fusion.60) | copy-start | bytes 12582916
  208.3 11.0 %collective-permute-start.9 = (f32[2,64,1,128]{3,1,2,0:T(8,128)S(1)}, f32[2,64,1,128]{3,1,2,0:T(8,128)S(1)}, u32[]{:S(2)}, u32[]{:S(2)}) collective-permute-start(f32[2,64,1,128]{3,1,2,0:T(8,128)S(1)} %get-tuple-element.77), channel_id=1, source_target_pairs={{0,8},{8,16},{16,24},{24,32},{32,40},{40,48},{48,56},{56,64},{64,7... | collective-permute-start | bytes 196616 | tf_op jit(solution)/shard_map/ppermute | solution.py:85
  210.9 8.3 %collective-permute-start.8 = (f32[2,64,1,128]{3,1,2,0:T(8,128)S(1)}, f32[2,64,1,128]{3,1,2,0:T(8,128)S(1)}, u32[]{:S(2)}, u32[]{:S(2)}) collective-permute-start(f32[2,64,1,128]{3,1,2,0:T(8,128)S(1)} %get-tuple-element.78), channel_id=1, source_target_pairs={{8,0},{16,8},{24,16},{32,24},{40,32},{48,40},{56,48},{64,56},{72,6... | collective-permute-start | bytes 196616 | tf_op jit(solution)/shard_map/ppermute | solution.py:86
  224.7 14.3 %copy-start.17 = (f32[1,256,256]{2,1,0:T(8,128)S(1)}, f32[1,256,256]{2,1,0:T(8,128)}, u32[]{:S(2)}) copy-start(f32[1,256,256]{2,1,0:T(8,128)} %param.18) | copy-start | bytes 786436
  232.7 19.4 %collective-permute-start.11 = (f32[2,64,66,1]{2,1,3,0:T(8,128)S(1)}, f32[2,64,66,1]{2,1,3,0:T(8,128)S(1)}, u32[]{:S(2)}, u32[]{:S(2)}) collective-permute-start(f32[2,64,66,1]{2,1,3,0:T(8,128)S(1)} %copy.46), channel_id=1, source_target_pairs={{0,1},{1,2},{2,3},{3,4},{4,5},{5,6},{6,7},{8,9},{9,10},{10,11},{11... | collective-permute-start | bytes 101384 | tf_op jit(solution)/shard_map/ppermute | solution.py:85
  233.9 13.3 %collective-permute-start.10 = (f32[2,64,66,1]{2,1,3,0:T(8,128)S(1)}, f32[2,64,66,1]{2,1,3,0:T(8,128)S(1)}, u32[]{:S(2)}, u32[]{:S(2)}) collective-permute-start(f32[2,64,66,1]{2,1,3,0:T(8,128)S(1)} %copy.44), channel_id=1, source_target_pairs={{1,0},{2,1},{3,2},{4,3},{5,4},{6,5},{7,6},{9,8},{10,9},{11,10},{12... | collective-permute-start | bytes 101384 | tf_op jit(solution)/shard_map/ppermute | solution.py:86
  256.8 20.5 %copy-start.11 = (f32[4096,256]{1,0:T(8,128)S(1)}, f32[4096,256]{1,0:T(8,128)}, u32[]{:S(2)}) copy-start(f32[4096,256]{1,0:T(8,128)} %divide_multiply_fusion) | copy-start | bytes 12582916
  256.8 20.5 %copy-start.14 = (f32[1,256,128]{2,1,0:T(8,128)S(1)}, f32[1,256,128]{2,1,0:T(8,128)}, u32[]{:S(2)}) copy-start(f32[1,256,128]{2,1,0:T(8,128)} %param.19) | copy-start | bytes 393220
  270.4 12.5 %copy-start.7 = (f32[2,64,64,128]{3,1,2,0:T(8,128)}, f32[2,64,64,128]{3,1,2,0:T(8,128)S(1)}, u32[]{:S(2)}) copy-start(f32[2,64,64,128]{3,1,2,0:T(8,128)S(1)} %fusion.19) | copy-start | bytes 12582916
  270.4 10.4 %collective-permute-start.13 = (f32[2,64,1,128]{3,1,2,0:T(8,128)S(1)}, f32[2,64,1,128]{3,1,2,0:T(8,128)S(1)}, u32[]{:S(2)}, u32[]{:S(2)}) collective-permute-start(f32[2,64,1,128]{3,1,2,0:T(8,128)S(1)} %get-tuple-element.75), channel_id=1, source_target_pairs={{0,8},{8,16},{16,24},{24,32},{32,40},{40,48},{48,56},{56,64},{64,7... | collective-permute-start | bytes 196616 | tf_op jit(solution)/shard_map/ppermute | solution.py:85
  275.2 7.1 %collective-permute-start.12 = (f32[2,64,1,128]{3,1,2,0:T(8,128)S(1)}, f32[2,64,1,128]{3,1,2,0:T(8,128)S(1)}, u32[]{:S(2)}, u32[]{:S(2)}) collective-permute-start(f32[2,64,1,128]{3,1,2,0:T(8,128)S(1)} %get-tuple-element.76), channel_id=1, source_target_pairs={{8,0},{16,8},{24,16},{32,24},{40,32},{48,40},{56,48},{64,56},{72,6... | collective-permute-start | bytes 196616 | tf_op jit(solution)/shard_map/ppermute | solution.py:86
  295.6 61.9 %collective-permute-start.15 = (f32[2,64,66,1]{2,1,3,0:T(8,128)S(1)}, f32[2,64,66,1]{2,1,3,0:T(8,128)S(1)}, u32[]{:S(2)}, u32[]{:S(2)}) collective-permute-start(f32[2,64,66,1]{2,1,3,0:T(8,128)S(1)} %copy.50), channel_id=1, source_target_pairs={{0,1},{1,2},{2,3},{3,4},{4,5},{5,6},{6,7},{8,9},{9,10},{10,11},{11... | collective-permute-start | bytes 101384 | tf_op jit(solution)/shard_map/ppermute | solution.py:85
  296.9 55.8 %collective-permute-start.14 = (f32[2,64,66,1]{2,1,3,0:T(8,128)S(1)}, f32[2,64,66,1]{2,1,3,0:T(8,128)S(1)}, u32[]{:S(2)}, u32[]{:S(2)}) collective-permute-start(f32[2,64,66,1]{2,1,3,0:T(8,128)S(1)} %copy.48), channel_id=1, source_target_pairs={{1,0},{2,1},{3,2},{4,3},{5,4},{6,5},{7,6},{9,8},{10,9},{11,10},{12... | collective-permute-start | bytes 101384 | tf_op jit(solution)/shard_map/ppermute | solution.py:86
  (10 other events, 64.4 us)

commit v2 on v0

v2 whole, which is shorter than its diff:
```python
import functools

import jax
import jax.numpy as jnp
from jax import lax
from jax.experimental import pallas as pl
from jax.experimental.pallas import tpu as pltpu
from jax.sharding import PartitionSpec as P

PASSES = 4
LOGICAL = pl.DeviceIdType.LOGICAL
F32 = jnp.float32
BF16 = jnp.bfloat16

LEVELS = 64
FEATURES = 128
WX = 64
WY = 128
CAP = 32
DEVICES = 128
ACTIVE = 2048
ROWS_X = WX + 8
ROWS_Y = WY + 32
GROUP = 16
GROUPS = DEVICES // GROUP


def slot_kernel(regime_ref, column_ref, pick_ref, slot_ref):
    width = 256
    blocks = ACTIVE // width
    expert = lax.broadcasted_iota(jnp.int32, (DEVICES, width), 0)
    earlier = lax.broadcasted_iota(jnp.int32, (width, width), 0)
    later = lax.broadcasted_iota(jnp.int32, (width, width), 1)
    upper = (earlier < later).astype(BF16)
    place = lax.broadcasted_iota(jnp.int32, (CAP, width), 0)
    counts = jnp.zeros((DEVICES, 1), F32)
    pick_x = jnp.zeros((CAP, DEVICES), F32)
    pick_y = jnp.zeros((CAP, DEVICES), F32)
    for block in range(blocks):
        part = slice(block * width, (block + 1) * width)
        named = regime_ref[:, part]
        column = column_ref[:, part]
        hit = (expert == named).astype(F32)
        hit16 = hit.astype(BF16)
        before = jnp.dot(hit16, upper, preferred_element_type=F32) + counts
        rank = jnp.sum(before * hit, axis=0, keepdims=True).astype(jnp.int32)
        counts = counts + jnp.sum(hit, axis=1, keepdims=True)
        slot_ref[:, part] = named * CAP + rank
        chosen = (place == rank).astype(F32)
        x = (column // WY).astype(F32)
        y = (column % WY).astype(F32)
        dims = (((1,), (1,)), ((), ()))
        pick_x = pick_x + lax.dot_general((chosen * x).astype(BF16), hit16, dims, preferred_element_type=F32)
        pick_y = pick_y + lax.dot_general((chosen * y).astype(BF16), hit16, dims, preferred_element_type=F32)
    pick_ref[...] = (pick_x * WY + pick_y).astype(jnp.int32)


def find_slots(regimes, active_columns):
    vmem = pl.BlockSpec(memory_space=pltpu.VMEM)
    return pl.pallas_call(
        slot_kernel,
        out_shape=(
            jax.ShapeDtypeStruct((CAP, DEVICES), jnp.int32),
            jax.ShapeDtypeStruct((1, ACTIVE), jnp.int32),
        ),
        in_specs=[vmem, vmem],
        out_specs=(vmem, vmem),
    )(regimes.reshape(1, ACTIVE), active_columns.reshape(1, ACTIVE))


NEIGHBOURS = [(dx, dy) for dx in (-1, 0, 1) for dy in (-1, 0, 1) if (dx, dy) != (0, 0)]


def split(value):
    high = value.astype(BF16)
    return high, (value - high.astype(F32)).astype(BF16)


def product(rows, high_ref, low_ref):
    high, low = split(rows)
    total = jnp.dot(high, low_ref[...], preferred_element_type=F32)
    total = total + jnp.dot(low, high_ref[...], preferred_element_type=F32)
    return total + jnp.dot(high, high_ref[...], preferred_element_type=F32)


def silu(z):
    half = 0.5 * z
    return half + half * jnp.tanh(half)


def main_kernel(
    pick_ref,
    u_hbm,
    v_hbm,
    d_hbm,
    w1_hbm,
    w2_hbm,
    w3_hbm,
    w4_hbm,
    drag_ref,
    diffused_ref,
    fields,
    profiles,
    state,
    dext,
    dwide,
    send,
    recv,
    answer,
    w1,
    w2,
    w3,
    w4,
    w1h,
    w1l,
    w2h,
    w2l,
    w3h,
    w3l,
    w4h,
    w4l,
    load_sem,
    own_sem,
    weight_sem,
    halo_send,
    halo_recv,
    dhalo_send,
    dhalo_recv,
    out_send,
    out_recv,
    back_send,
    back_recv,
):
    tile = lax.axis_index("tile")
    inf = lax.axis_index("inf")
    me = tile * 8 + inf
    at_x, at_z = tile // 4, tile % 4
    at_y, at_c = inf // 2, inf % 2

    pieces = 4
    wide = WX // pieces
    loads = []
    for piece in range(pieces):
        part = pl.ds(piece * wide, wide)
        for which, source in enumerate((u_hbm, v_hbm)):
            loads.append(
                pltpu.make_async_copy(source.at[:, part, :], fields.at[which, :, part, :], load_sem.at[piece, which])
            )
    own_d = pltpu.make_async_copy(d_hbm, dext.at[1, pl.ds(8, WX), :], own_sem)
    weight_loads = [
        pltpu.make_async_copy(source.at[0], target, weight_sem.at[number])
        for number, (source, target) in enumerate(((w1_hbm, w1), (w2_hbm, w2), (w3_hbm, w3), (w4_hbm, w4)))
    ]
    for load in loads:
        load.start()
    own_d.start()
    for load in weight_loads:
        load.start()

    barrier = pltpu.get_barrier_semaphore()

    def greet(step, carry):
        other = me + step
        other = jnp.where(other >= DEVICES, other - DEVICES, other)
        pl.semaphore_signal(barrier, inc=1, device_id=other, device_id_type=LOGICAL)
        return carry

    lax.fori_loop(1, DEVICES, greet, 0)

    flat_fields = fields.reshape(2 * LEVELS * WX, WY)

    def turn(x, carry):
        block = flat_fields[pl.ds(x, FEATURES, stride=WX), :]
        block = block.T
        state[0, x + 4, 16 : 16 + WY, :] = block
        profiles[pl.ds(pl.multiple_of(x * WY, WY), WY), :] = block
        return carry

    for piece in range(pieces):
        loads[2 * piece].wait()
        loads[2 * piece + 1].wait()
        lax.fori_loop(piece * wide, (piece + 1) * wide, turn, 0)
    own_d.wait()

    @pl.when(tile == 0)
    def _():
        state[0, 0:4, 8 : 24 + WY, :] = jnp.zeros((4, WY + 16, FEATURES), F32)
        dext[:, 0:8, :] = jnp.zeros((3, 8, WY), F32)

    @pl.when(tile == 15)
    def _():
        state[0, WX + 4 : WX + 8, 8 : 24 + WY, :] = jnp.zeros((4, WY + 16, FEATURES), F32)
        dext[:, WX + 8 : WX + 16, :] = jnp.zeros((3, 8, WY), F32)

    @pl.when(inf == 0)
    def _():
        state[0, :, 8:16, :] = jnp.zeros((ROWS_X, 8, FEATURES), F32)
        dext[0, :, :] = jnp.zeros((WX + 16, WY), F32)

    @pl.when(inf == 7)
    def _():
        state[0, :, 16 + WY : 24 + WY, :] = jnp.zeros((ROWS_X, 8, FEATURES), F32)
        dext[2, :, :] = jnp.zeros((WX + 16, WY), F32)

    pl.semaphore_wait(barrier, DEVICES - 1)

    def halo(number):
        dx, dy = NEIGHBOURS[number]
        opposite = NEIGHBOURS.index((-dx, -dy))
        there_x, there_y = tile + dx, inf + dy
        exists = (there_x >= 0) & (there_x < 16) & (there_y >= 0) & (there_y < 8)
        comes_x, comes_y = tile - dx, inf - dy
        comes = (comes_x >= 0) & (comes_x < 16) & (comes_y >= 0) & (comes_y < 8)
        from_x = {1: pl.ds(WX, 4), -1: pl.ds(4, 4), 0: pl.ds(4, WX)}[dx]
        to_x = {1: pl.ds(0, 4), -1: pl.ds(WX + 4, 4), 0: pl.ds(4, WX)}[dx]
        from_y = {1: pl.ds(8 + WY, 8), -1: pl.ds(16, 8), 0: pl.ds(16, WY)}[dy]
        to_y = {1: pl.ds(8, 8), -1: pl.ds(16 + WY, 8), 0: pl.ds(16, WY)}[dy]
        from_d = {1: pl.ds(WX, 8), -1: pl.ds(8, 8), 0: pl.ds(8, WX)}[dx]
        to_d = {1: pl.ds(0, 8), -1: pl.ds(WX + 8, 8), 0: pl.ds(8, WX)}[dx]
        other = there_x * 8 + there_y
        profile = pltpu.make_async_remote_copy(
            src_ref=state.at[0, from_x, from_y, :],
            dst_ref=state.at[0, to_x, to_y, :],
            send_sem=halo_send.at[number],
            recv_sem=halo_recv.at[number],
            device_id=other,
            device_id_type=LOGICAL,
        )
        number_d = pltpu.make_async_remote_copy(
            src_ref=dext.at[1, from_d, :],
            dst_ref=dext.at[1 - dy, to_d, :],
            send_sem=dhalo_send.at[number],
            recv_sem=dhalo_recv.at[number],
            device_id=other,
            device_id_type=LOGICAL,
        )
        return exists, comes, profile, number_d

    for number in range(8):
        exists, _, profile, coefficient = halo(number)

        @pl.when(exists)
        def _():
            coefficient.start()
            profile.start()

    def target(turn_number, lane):
        x = (at_x + lane) % 4
        c = (at_c + lane // 4) % 2
        z = (at_z + lane + turn_number) % 4
        y = (at_y + lane + turn_number // 4) % 4
        return x * 32 + z * 8 + y * 2 + c

    def source(turn_number, lane):
        x = (at_x + 8 - lane) % 4
        c = (at_c + 2 - lane // 4) % 2
        z = (at_z + 24 - lane - turn_number) % 4
        y = (at_y + 12 - lane - turn_number // 4) % 4
        return x * 32 + z * 8 + y * 2 + c

    def away(step, other, group):
        return pltpu.make_async_remote_copy(
            src_ref=send.at[step],
            dst_ref=recv.at[step],
            send_sem=out_send,
            recv_sem=out_recv.at[group],
            device_id=other,
            device_id_type=LOGICAL,
        )

    def back(step, other):
        return pltpu.make_async_remote_copy(
            src_ref=answer.at[step],
            dst_ref=drag_ref.at[me],
            send_sem=back_send,
            recv_sem=back_recv,
            device_id=other,
            device_id_type=LOGICAL,
        )

    def dispatch(turn_number, carry):
        for lane in range(8):
            step = turn_number * 8 + lane
            other = target(turn_number, lane)
            for k in range(CAP):
                row = pick_ref[k, other]
                send[step, k : k + 1, :] = profiles[pl.ds(row, 1), :]
            if lane == 0:

                @pl.when(turn_number > 0)
                def _():
                    away(step, other, turn_number // 2).start()
            else:
                away(step, other, turn_number // 2).start()
        return carry

    lax.fori_loop(0, DEVICES // 8, dispatch, 0)
    recv[0] = send[0]

    for load in weight_loads:
        load.wait()
    for whole, high_ref, low_ref in ((w1, w1h, w1l), (w2, w2h, w2l), (w3, w3h, w3l), (w4, w4h, w4l)):
        high, low = split(whole[...])
        high_ref[...] = high
        low_ref[...] = low

    for number in range(8):
        exists, comes, profile, coefficient = halo(number)

        @pl.when(comes)
        def _():
            coefficient.wait_recv()
            profile.wait_recv()

        @pl.when(exists)
        def _():
            coefficient.wait_send()
            profile.wait_send()

    lane = lax.broadcasted_iota(jnp.int32, (WX + 16, WY), 1)
    left = pltpu.roll(dext[0], 8, 1)
    right = pltpu.roll(dext[2], 8, 1)
    sides = jnp.where(lane < 8, left, right)
    sides = jnp.concatenate([sides, jnp.zeros((WY - WX - 16, WY), F32)], axis=0).T[0:16, :]

    def widen(x, carry):
        row = dext[1, pl.ds(x + 4, 1), :]
        dwide[x, 16 : 16 + WY, :] = jnp.broadcast_to(row, (WY, FEATURES)).T
        column = pltpu.roll(sides, WY - 4 - x, 1)[:, 0:1]
        column = jnp.broadcast_to(column, (16, FEATURES))
        dwide[x, 8:16, :] = column[0:8]
        dwide[x, 16 + WY : 24 + WY, :] = column[8:16]
        return carry

    lax.fori_loop(1, ROWS_X - 1, widen, 0)

    def diffuse(number):
        held, following = number % 2, 1 - number % 2
        last = number == PASSES - 1
        first = number + 1
        count = (ROWS_X - 2 * first) // 2
        cuts = [(16 + 64 * cut, 64) for cut in range(2)] if last else [(8 + 48 * cut, 48) for cut in range(3)]

        def rows(step, carry):
            x = first + 2 * step
            for start, size in cuts:
                middle = [state[held, x - 1 + k, start : start + size, :] for k in range(4)]
                for k in range(2):
                    q = middle[k + 1]
                    near = middle[k] + middle[k + 2]
                    near = near + state[held, x + k, start - 1 : start + size - 1, :]
                    near = near + state[held, x + k, start + 1 : start + size + 1, :]
                    new = q + dwide[x + k, start : start + size, :] * (near - 4.0 * q)
                    if last:
                        diffused_ref[x + k - 4, start - 16 : start - 16 + size, :] = new
                    else:
                        state[following, x + k, start : start + size, :] = new
            return carry

        lax.fori_loop(0, count, rows, 0)

    def network(group, carry):
        rows = recv[pl.ds(group * GROUP, GROUP)].reshape(GROUP * CAP, FEATURES)
        center = jnp.mean(rows, axis=-1, keepdims=True)
        shifted = rows - center
        spread = jnp.mean(shifted * shifted, axis=-1, keepdims=True)
        rows = shifted * lax.rsqrt(spread + 1e-05)
        hidden = silu(product(rows, w1h, w1l))
        hidden = silu(product(hidden, w2h, w2l))
        hidden = silu(product(hidden, w3h, w3l))
        result = product(hidden, w4h, w4l)
        answer[pl.ds(group * GROUP, GROUP)] = result.reshape(GROUP, CAP, FEATURES)
        for part in range(2):
            for lane in range(8):
                turn_number = group * 2 + part
                step = turn_number * 8 + lane
                other = source(turn_number, lane)
                if part == 0 and lane == 0:

                    @pl.when(group > 0)
                    def _():
                        back(step, other).start()
                else:
                    back(step, other).start()
        return carry

    def arrived(first, count, group):
        pltpu.make_async_remote_copy(
            src_ref=recv.at[pl.ds(first, count)],
            dst_ref=recv.at[pl.ds(first, count)],
            send_sem=out_send,
            recv_sem=out_recv.at[group],
            device_id=me,
            device_id_type=LOGICAL,
        ).wait_recv()

    def arrived_network(group, carry):
        arrived(group * GROUP, GROUP, group)
        return network(group, carry)

    for number in range(2):
        diffuse(number)
    arrived(1, GROUP - 1, 0)
    network(0, 0)
    drag_ref[me] = answer[0]
    lax.fori_loop(1, 4, arrived_network, 0)
    for number in range(2, PASSES):
        diffuse(number)
    lax.fori_loop(4, GROUPS, arrived_network, 0)

    others = DEVICES - 1
    pltpu.make_async_remote_copy(
        src_ref=answer.at[pl.ds(0, others)],
        dst_ref=drag_ref.at[pl.ds(0, others)],
        send_sem=back_send,
        recv_sem=back_recv,
        device_id=me,
        device_id_type=LOGICAL,
    ).wait()
    pltpu.make_async_remote_copy(
        src_ref=send.at[pl.ds(0, others)],
        dst_ref=recv.at[pl.ds(0, others)],
        send_sem=out_send,
        recv_sem=out_recv.at[0],
        device_id=me,
        device_id_type=LOGICAL,
    ).wait_send()


def drag_and_diffusion(pick, u_field, v_field, diffusivity, layers):
    vmem = pl.BlockSpec(memory_space=pltpu.VMEM)
    smem = pl.BlockSpec(memory_space=pltpu.SMEM)
    hbm = pl.BlockSpec(memory_space=pl.ANY)
    shapes = [layer.shape[1:] for layer in layers]
    halves = [pltpu.VMEM(shape, BF16) for shape in shapes for _ in range(2)]
    dma = pltpu.SemaphoreType.DMA
    return pl.pallas_call(
        main_kernel,
        out_shape=(
            jax.ShapeDtypeStruct((DEVICES, CAP, FEATURES), F32),
            jax.ShapeDtypeStruct((WX, WY, FEATURES), F32),
        ),
        in_specs=[smem] + [hbm] * 7,
        out_specs=(vmem, vmem),
        scratch_shapes=[
            pltpu.VMEM((2, LEVELS, WX, WY), F32),
            pltpu.VMEM((WX * WY, FEATURES), F32),
            pltpu.VMEM((2, ROWS_X, ROWS_Y, FEATURES), F32),
            pltpu.VMEM((3, WX + 16, WY), F32),
            pltpu.VMEM((ROWS_X, ROWS_Y, FEATURES), F32),
            pltpu.VMEM((DEVICES, CAP, FEATURES), F32),
            pltpu.VMEM((DEVICES, CAP, FEATURES), F32),
            pltpu.VMEM((DEVICES, CAP, FEATURES), F32),
            *[pltpu.VMEM(shape, F32) for shape in shapes],
            *halves,
            dma((4, 2)),
            dma,
            dma((4,)),
            dma((8,)),
            dma((8,)),
            dma((8,)),
            dma((8,)),
            dma,
            dma((GROUPS,)),
            dma,
            dma,
        ],
        compiler_params=pltpu.CompilerParams(
            collective_id=0, has_side_effects=True, vmem_limit_bytes=50 << 20
        ),
    )(pick, u_field, v_field, diffusivity, *layers)


def place_kernel(column_ref, slot_ref, drag_ref, diffused_ref, u_hbm, v_hbm, dense, staged, out_sem):
    def clear(x, carry):
        dense[pl.ds(x * WY, WY), :] = jnp.zeros((WY, FEATURES), F32)
        return carry

    lax.fori_loop(0, WX, clear, 0)
    drags = drag_ref.reshape(DEVICES * CAP, FEATURES)

    def place(step, carry):
        for k in range(16):
            row = step * 16 + k
            dense[pl.ds(column_ref[row], 1), :] = drags[pl.ds(slot_ref[0, row], 1), :]
        return carry

    lax.fori_loop(0, ACTIVE // 16, place, 0)
    flat = staged.reshape(2 * LEVELS * WX, WY)

    def turn(x, carry):
        block = dense[pl.ds(x * WY, WY), :] + diffused_ref[x]
        flat[pl.ds(x, FEATURES, stride=WX), :] = block.T
        return carry

    pieces = 4
    wide = WX // pieces
    copies = []
    for piece in range(pieces):
        lax.fori_loop(piece * wide, (piece + 1) * wide, turn, 0)
        part = pl.ds(piece * wide, wide)
        for which, target in enumerate((u_hbm, v_hbm)):
            copy = pltpu.make_async_copy(staged.at[which, :, part, :], target.at[:, part, :], out_sem.at[piece, which])
            copy.start()
            copies.append(copy)
    for copy in copies:
        copy.wait()


def place_drag(active_columns, slots, drag, diffused):
    vmem = pl.BlockSpec(memory_space=pltpu.VMEM)
    smem = pl.BlockSpec(memory_space=pltpu.SMEM)
    hbm = pl.BlockSpec(memory_space=pl.ANY)
    shape = jax.ShapeDtypeStruct((LEVELS, WX, WY), F32)
    return pl.pallas_call(
        place_kernel,
        out_shape=(shape, shape),
        in_specs=[smem, smem, vmem, vmem],
        out_specs=(hbm, hbm),
        scratch_shapes=[
            pltpu.VMEM((WX * WY, FEATURES), F32),
            pltpu.VMEM((2, LEVELS, WX, WY), F32),
            pltpu.SemaphoreType.DMA((4, 2)),
        ],
        compiler_params=pltpu.CompilerParams(vmem_limit_bytes=30 << 20),
    )(active_columns, slots, drag, diffused)


def body(
    u_field,
    v_field,
    diffusivity,
    active_columns,
    regimes,
    first_layer,
    second_layer,
    third_layer,
    last_layer,
):
    pick, slots = find_slots(regimes, active_columns)
    layers = (first_layer, second_layer, third_layer, last_layer)
    drag, diffused = drag_and_diffusion(pick, u_field, v_field, diffusivity, layers)
    return place_drag(active_columns, slots, drag, diffused)


def solution(mesh):
    in_specs = (
        P(None, "tile", "inf"),
        P(None, "tile", "inf"),
        P("tile", "inf"),
        P(("tile", "inf")),
        P(("tile", "inf"), None),
        P(("tile", "inf"), None, None),
        P(("tile", "inf"), None, None),
        P(("tile", "inf"), None, None),
        P(("tile", "inf"), None, None),
    )
    out_specs = (P(None, "tile", "inf"), P(None, "tile", "inf"))
    return jax.shard_map(body, mesh=mesh, in_specs=in_specs, out_specs=out_specs, check_vma=False)
```

time: 396 us -> 118 us (0.30)
  the two profiles are of different devices: /device:TPU:3 before, /device:TPU:1 now
where the time goes in v2:
time: 118 us
  Pallas kernels  109 us (92%)
  local copies, waits for them, and re-layouts  7.37 us (6%)
    pallas_call x1, Pallas kernels, drag_and_diffusion(): pl.pallas_call(main_kernel, out_shape=(jax.ShapeDtypeStruct((DEVICES, CAP...  92.4 us
    pallas_call x1, Pallas kernels, place_drag(): pl.pallas_call(place_kernel, out_shape=(shape, shape), in_specs=[smem, sm...  14.1 us
    unnamed x18, local copies, waits for them, and re-layouts  7.37 us
    pallas_call x1, Pallas kernels, find_slots(): pl.pallas_call(slot_kernel, out_shape=(jax.ShapeDtypeStruct((CAP, DEVICES...  2.97 us

profile of v2, /device:TPU:1, one launch (start us, length us, event | category | flops | bytes accessed | tf_op | source)
XLA Modules:
  0.0 117.5 jit_solution(12964301775563566463)
XLA Ops:
  0.6 3.0 %shard_map.104 = (s32[32,128]{1,0:T(8,128)}, s32[1,2048]{1,0:T(1,128)}) custom-call(s32[1,2048]{1,0:T(1,128)} %bitcast.3, s32[1,2048]{1,0:T(1,128)} %bitcast.2), custom_call_target="tpu_custom_call" | custom-call | tf_op jit(solution)/shard_map/pallas_call | solution.py:60
  3.6 0.0 copy-start.1
  3.6 0.9 copy-done.1
  4.6 0.0 copy-start.2
  4.6 0.9 copy-done.2
  5.5 0.0 copy-start.3
  5.5 0.9 copy-done.3
  6.4 0.0 copy-start.4
  6.4 0.9 copy-done.4
  7.3 0.0 copy-start.5
  7.3 0.8 copy-done.5
  8.1 0.0 copy-start.7
  8.1 0.7 copy-done.7
  8.8 0.0 copy-start.6
  8.8 0.0 copy-start.8
  8.8 92.4 %shard_map.105 = (f32[128,32,128]{2,1,0:T(8,128)S(1)}, f32[64,128,128]{2,1,0:T(8,128)}) custom-call(s32[32,128]{1,0:T(8,128)S(1)} %copy-done.7, f32[64,64,128]{2,1,0:T(8,128)} %u_hbm.1, f32[64,64,128]{2,1,0:T(8,128)} %v_hbm.1, f32[64,128]{1,0:T(8,128)S(1)} %copy-done.5, f32[1,128,256]{2,1,0:T(8,128)S(1)} %copy-done.3, f32[1,256,256]{2,1,0:T(8,128)S(1)} %copy-done.1, ...), custom_call_target="tpu_custom_call" | custom-call | tf_op jit(solution)/shard_map/pallas_call | solution.py:437
  101.2 0.0 copy-done.6
  101.2 0.0 copy-done.8
  101.2 0.0 copy-start
  101.3 2.2 %copy-done = f32[64,128,128]{2,1,0:T(8,128)S(1)} copy-done((f32[64,128,128]{2,1,0:T(8,128)S(1)}, f32[64,128,128]{2,1,0:T(8,128)}, u32[]{:S(2)}) %copy-start) | copy-done | bytes 4194328
  103.4 14.1 %shard_map.106 = (f32[64,64,128]{2,1,0:T(8,128)}, f32[64,64,128]{2,1,0:T(8,128)}) custom-call(s32[2048]{0:T(1024)S(1)} %copy-done.6, s32[1,2048]{1,0:T(1,128)S(1)} %copy-done.8, f32[128,32,128]{2,1,0:T(8,128)S(1)} %get-tuple-element.8.drag_ref, f32[64,128,128]{2,1,0:T(8,128)S(1)} %copy-done), custom_call_target="tpu_custom_call" | custom-call | tf_op jit(solution)/shard_map/pallas_call | solution.py:515
Async XLA Ops:
  3.6 1.0 copy-start.1
  4.6 0.9 copy-start.2
  5.5 0.9 copy-start.3
  6.4 0.9 copy-start.4
  7.3 0.8 copy-start.5
  8.1 0.7 copy-start.7
  8.8 92.4 %copy-start.6 = (s32[2048]{0:T(1024)S(1)}, s32[2048]{0:T(1024)}, u32[]{:S(2)}) copy-start(s32[2048]{0:T(1024)} %column_ref.1) | copy-start | bytes 24580
  8.8 92.4 %copy-start.8 = (s32[1,2048]{1,0:T(1,128)S(1)}, s32[1,2048]{1,0:T(1,128)}, u32[]{:S(2)}) copy-start(s32[1,2048]{1,0:T(1,128)} %get-tuple-element.6.slot_ref) | copy-start | bytes 24580
  101.2 2.2 %copy-start = (f32[64,128,128]{2,1,0:T(8,128)S(1)}, f32[64,128,128]{2,1,0:T(8,128)}, u32[]{:S(2)}) copy-start(f32[64,128,128]{2,1,0:T(8,128)} %get-tuple-element.9.diffused_ref) | copy-start | bytes 12582916

commit v3 on v2

--- a/solution.py
+++ b/solution.py
@@ -98,11 +98,12 @@
     w3_hbm,
     w4_hbm,
     drag_ref,
-    diffused_ref,
+    diffused_hbm,
     fields,
     profiles,
     state,
     dext,
+    sides_ref,
     dwide,
     send,
     recv,
@@ -130,6 +131,7 @@
     out_recv,
     back_send,
     back_recv,
+    diffused_sem,
 ):
     tile = lax.axis_index("tile")
     inf = lax.axis_index("inf")
@@ -159,27 +161,36 @@
 
     barrier = pltpu.get_barrier_semaphore()
 
-    def greet(step, carry):
+    def greet(step):
         other = me + step
         other = jnp.where(other >= DEVICES, other - DEVICES, other)
         pl.semaphore_signal(barrier, inc=1, device_id=other, device_id_type=LOGICAL)
-        return carry
-
-    lax.fori_loop(1, DEVICES, greet, 0)
 
     flat_fields = fields.reshape(2 * LEVELS * WX, WY)
 
-    def turn(x, carry):
-        block = flat_fields[pl.ds(x, FEATURES, stride=WX), :]
-        block = block.T
-        state[0, x + 4, 16 : 16 + WY, :] = block
-        profiles[pl.ds(pl.multiple_of(x * WY, WY), WY), :] = block
+    def turn(step, carry):
+        for k in range(4):
+            x = 4 * step + k
+            if k < 3:
+                greet(2 * x + 1)
+                greet(2 * x + 2)
+            block = flat_fields[pl.ds(x, FEATURES, stride=WX), :].T
+            state[0, x + 4, 16 : 16 + WY, :] = block
+            profiles[pl.ds(pl.multiple_of(x * WY, WY), WY), :] = block
+        x = 4 * step + 3
+
+        greet(2 * x + 1)
+
+        @pl.when(step < WX // 4 - 1)
+        def _():
+            greet(2 * x + 2)
+
         return carry
 
     for piece in range(pieces):
         loads[2 * piece].wait()
         loads[2 * piece + 1].wait()
-        lax.fori_loop(piece * wide, (piece + 1) * wide, turn, 0)
+        lax.fori_loop(piece * wide // 4, (piece + 1) * wide // 4, turn, 0)
     own_d.wait()
 
     @pl.when(tile == 0)
@@ -304,35 +315,36 @@
         high_ref[...] = high
         low_ref[...] = low
 
-    for number in range(8):
-        exists, comes, profile, coefficient = halo(number)
-
-        @pl.when(comes)
-        def _():
-            coefficient.wait_recv()
-            profile.wait_recv()
-
-        @pl.when(exists)
-        def _():
-            coefficient.wait_send()
-            profile.wait_send()
-
-    lane = lax.broadcasted_iota(jnp.int32, (WX + 16, WY), 1)
-    left = pltpu.roll(dext[0], 8, 1)
-    right = pltpu.roll(dext[2], 8, 1)
-    sides = jnp.where(lane < 8, left, right)
-    sides = jnp.concatenate([sides, jnp.zeros((WY - WX - 16, WY), F32)], axis=0).T[0:16, :]
-
-    def widen(x, carry):
-        row = dext[1, pl.ds(x + 4, 1), :]
-        dwide[x, 16 : 16 + WY, :] = jnp.broadcast_to(row, (WY, FEATURES)).T
-        column = pltpu.roll(sides, WY - 4 - x, 1)[:, 0:1]
-        column = jnp.broadcast_to(column, (16, FEATURES))
-        dwide[x, 8:16, :] = column[0:8]
-        dwide[x, 16 + WY : 24 + WY, :] = column[8:16]
-        return carry
-
-    lax.fori_loop(1, ROWS_X - 1, widen, 0)
+    def receive_halo():
+        for number in range(8):
+            exists, comes, profile, coefficient = halo(number)
+
+            @pl.when(comes)
+            def _():
+                coefficient.wait_recv()
+                profile.wait_recv()
+
+            @pl.when(exists)
+            def _():
+                coefficient.wait_send()
+                profile.wait_send()
+
+        lane = lax.broadcasted_iota(jnp.int32, (WX + 16, WY), 1)
+        left = pltpu.roll(dext[0], 8, 1)
+        right = pltpu.roll(dext[2], 8, 1)
+        sides = jnp.where(lane < 8, left, right)
+        sides_ref[...] = jnp.concatenate([sides, jnp.zeros((WY - WX - 16, WY), F32)], axis=0).T[0:16, :]
+
+    def widen(step, carry):
+        for k in range(4):
+            x = 4 * step + k
+            row = dext[1, pl.ds(x + 4, 1), :]
+            dwide[x, 16 : 16 + WY, :] = jnp.broadcast_to(row, (WY, FEATURES)).T
+            column = pltpu.roll(sides_ref[...], WY - 4 - x, 1)[:, 0:1]
+            column = jnp.broadcast_to(column, (16, FEATURES))
+            dwide[x, 8:16, :] = column[0:8]
+            dwide[x, 16 + WY : 24 + WY, :] = column[8:16]
+        return carry
 
     def diffuse(number):
         held, following = number % 2, 1 - number % 2
@@ -352,7 +364,8 @@
                     near = near + state[held, x + k, start + 1 : start + size + 1, :]
                     new = q + dwide[x + k, start : start + size, :] * (near - 4.0 * q)
                     if last:
-                        diffused_ref[x + k - 4, start - 16 : start - 16 + size, :] = new
+                        at = pl.multiple_of((x + k - 4) * WY, WY) + start - 16
+                        profiles[pl.ds(pl.multiple_of(at, 8), size), :] = new
                     else:
                         state[following, x + k, start : start + size, :] = new
             return carry
@@ -395,18 +408,41 @@
         ).wait_recv()
 
     def arrived_network(group, carry):
-        arrived(group * GROUP, GROUP, group)
-        return network(group, carry)
-
-    for number in range(2):
-        diffuse(number)
-    arrived(1, GROUP - 1, 0)
-    network(0, 0)
+        @pl.when(group == 0)
+        def _():
+            arrived(1, GROUP - 1, 0)
+
+        @pl.when(group > 0)
+        def _():
+            arrived(group * GROUP, GROUP, group)
+
+        network(group, carry)
+
+        @pl.when(group == 1)
+        def _():
+            receive_halo()
+            lax.fori_loop(0, ROWS_X // 8, widen, 0)
+
+        @pl.when(group == 3)
+        def _():
+            lax.fori_loop(ROWS_X // 8, ROWS_X // 4, widen, 0)
+
+        @pl.when(group == 4)
+        def _():
+            diffuse(0)
+
+        @pl.when(group == 5)
+        def _():
+            diffuse(1)
+
+        return carry
+
+    lax.fori_loop(0, GROUPS, arrived_network, 0)
     drag_ref[me] = answer[0]
-    lax.fori_loop(1, 4, arrived_network, 0)
-    for number in range(2, PASSES):
-        diffuse(number)
-    lax.fori_loop(4, GROUPS, arrived_network, 0)
+    diffuse(2)
+    diffuse(3)
+    diffused = pltpu.make_async_copy(profiles, diffused_hbm, diffused_sem)
+    diffused.start()
 
     others = DEVICES - 1
     pltpu.make_async_remote_copy(
@@ -425,12 +461,13 @@
         device_id=me,
         device_id_type=LOGICAL,
     ).wait_send()
+    diffused.wait()
 
 
 def drag_and_diffusion(pick, u_field, v_field, diffusivity, layers):
     vmem = pl.BlockSpec(memory_space=pltpu.VMEM)
     smem = pl.BlockSpec(memory_space=pltpu.SMEM)
-    hbm = pl.BlockSpec(memory_space=pl.ANY)
+    hbm = pl.BlockSpec(memory_space=pltpu.HBM)
     shapes = [layer.shape[1:] for layer in layers]
     halves = [pltpu.VMEM(shape, BF16) for shape in shapes for _ in range(2)]
     dma = pltpu.SemaphoreType.DMA
@@ -438,15 +475,16 @@
         main_kernel,
         out_shape=(
             jax.ShapeDtypeStruct((DEVICES, CAP, FEATURES), F32),
-            jax.ShapeDtypeStruct((WX, WY, FEATURES), F32),
+            jax.ShapeDtypeStruct((WX * WY, FEATURES), F32),
         ),
         in_specs=[smem] + [hbm] * 7,
-        out_specs=(vmem, vmem),
+        out_specs=(vmem, hbm),
         scratch_shapes=[
             pltpu.VMEM((2, LEVELS, WX, WY), F32),
             pltpu.VMEM((WX * WY, FEATURES), F32),
             pltpu.VMEM((2, ROWS_X, ROWS_Y, FEATURES), F32),
             pltpu.VMEM((3, WX + 16, WY), F32),
+            pltpu.VMEM((16, WY), F32),
             pltpu.VMEM((ROWS_X, ROWS_Y, FEATURES), F32),
             pltpu.VMEM((DEVICES, CAP, FEATURES), F32),
             pltpu.VMEM((DEVICES, CAP, FEATURES), F32),
@@ -464,40 +502,54 @@
             dma((GROUPS,)),
             dma,
             dma,
+            dma,
         ],
         compiler_params=pltpu.CompilerParams(
-            collective_id=0, has_side_effects=True, vmem_limit_bytes=50 << 20
+            collective_id=0, has_side_effects=True, vmem_limit_bytes=59840 << 10
         ),
     )(pick, u_field, v_field, diffusivity, *layers)
 
 
-def place_kernel(column_ref, slot_ref, drag_ref, diffused_ref, u_hbm, v_hbm, dense, staged, out_sem):
+def place_kernel(
+    column_ref, slot_ref, drag_ref, diffused_hbm, u_hbm, v_hbm, dense, diffused, staged, in_sem, out_sem
+):
+    pieces = 4
+    wide = WX // pieces
+    loads = []
+    for piece in range(pieces):
+        part = pl.ds(piece * wide * WY, wide * WY)
+        load = pltpu.make_async_copy(diffused_hbm.at[part], diffused.at[part], in_sem.at[piece])
+        load.start()
+        loads.append(load)
+
     def clear(x, carry):
-        dense[pl.ds(x * WY, WY), :] = jnp.zeros((WY, FEATURES), F32)
+        dense[pl.ds(pl.multiple_of(x * WY, WY), WY), :] = jnp.zeros((WY, FEATURES), F32)
         return carry
 
     lax.fori_loop(0, WX, clear, 0)
     drags = drag_ref.reshape(DEVICES * CAP, FEATURES)
 
     def place(step, carry):
+        rows = [drags[pl.ds(slot_ref[0, step * 16 + k], 1), :] for k in range(16)]
         for k in range(16):
-            row = step * 16 + k
-            dense[pl.ds(column_ref[row], 1), :] = drags[pl.ds(slot_ref[0, row], 1), :]
+            dense[pl.ds(column_ref[step * 16 + k], 1), :] = rows[k]
         return carry
 
     lax.fori_loop(0, ACTIVE // 16, place, 0)
     flat = staged.reshape(2 * LEVELS * WX, WY)
 
-    def turn(x, carry):
-        block = dense[pl.ds(x * WY, WY), :] + diffused_ref[x]
-        flat[pl.ds(x, FEATURES, stride=WX), :] = block.T
-        return carry
-
-    pieces = 4
-    wide = WX // pieces
+    def turn(step, carry):
+        for k in range(4):
+            x = 4 * step + k
+            part = pl.ds(pl.multiple_of(x * WY, WY), WY)
+            block = dense[part, :] + diffused[part, :]
+            flat[pl.ds(x, FEATURES, stride=WX), :] = block.T
+        return carry
+
     copies = []
     for piece in range(pieces):
-        lax.fori_loop(piece * wide, (piece + 1) * wide, turn, 0)
+        loads[piece].wait()
+        lax.fori_loop(piece * wide // 4, (piece + 1) * wide // 4, turn, 0)
         part = pl.ds(piece * wide, wide)
         for which, target in enumerate((u_hbm, v_hbm)):
             copy = pltpu.make_async_copy(staged.at[which, :, part, :], target.at[:, part, :], out_sem.at[piece, which])
@@ -510,19 +562,21 @@
 def place_drag(active_columns, slots, drag, diffused):
     vmem = pl.BlockSpec(memory_space=pltpu.VMEM)
     smem = pl.BlockSpec(memory_space=pltpu.SMEM)
-    hbm = pl.BlockSpec(memory_space=pl.ANY)
+    hbm = pl.BlockSpec(memory_space=pltpu.HBM)
     shape = jax.ShapeDtypeStruct((LEVELS, WX, WY), F32)
     return pl.pallas_call(
         place_kernel,
         out_shape=(shape, shape),
-        in_specs=[smem, smem, vmem, vmem],
+        in_specs=[smem, smem, vmem, hbm],
         out_specs=(hbm, hbm),
         scratch_shapes=[
             pltpu.VMEM((WX * WY, FEATURES), F32),
+            pltpu.VMEM((WX * WY, FEATURES), F32),
             pltpu.VMEM((2, LEVELS, WX, WY), F32),
+            pltpu.SemaphoreType.DMA((4,)),
             pltpu.SemaphoreType.DMA((4, 2)),
         ],
-        compiler_params=pltpu.CompilerParams(vmem_limit_bytes=30 << 20),
+        compiler_params=pltpu.CompilerParams(vmem_limit_bytes=59840 << 10),
     )(active_columns, slots, drag, diffused)
 
 

time: 118 us -> 97.5 us (0.83)
  Pallas kernels: 109 us -> 96.4 us
  local copies, waits for them, and re-layouts: 7.37 us -> 0 us
    pallas_call x1, Pallas kernels: 92.4 us -> 83.3 us  [drag_and_diffusion(): pl.pallas_call(main_kernel, out_shape=(jax.ShapeDtypeStruct((DEVICES, CAP...]
    unnamed x18 -> x0, local copies, waits for them, and re-layouts: 7.37 us -> none
    pallas_call x1, Pallas kernels: 14.1 us -> 10.2 us  [place_drag(): pl.pallas_call(place_kernel, out_shape=(shape, shape), in_specs=[smem, sm...]
where the time goes in v3:
time: 97.5 us; the launch traced here: 97.1 us
  Pallas kernels  96.4 us (99%)
    pallas_call x1, Pallas kernels, drag_and_diffusion(): pl.pallas_call(main_kernel, out_shape=(jax.ShapeDtypeStruct((DEVICES, CAP...  83.3 us
    pallas_call x1, Pallas kernels, place_drag(): pl.pallas_call(place_kernel, out_shape=(shape, shape), in_specs=[smem, sm...  10.2 us
    pallas_call x1, Pallas kernels, find_slots(): pl.pallas_call(slot_kernel, out_shape=(jax.ShapeDtypeStruct((CAP, DEVICES...  2.97 us

profile of v3, /device:TPU:1, one launch (start us, length us, event | category | flops | bytes accessed | tf_op | source)
XLA Modules:
  0.0 97.1 jit_solution(16182571262045402785)
XLA Ops:
  0.6 3.0 %shard_map.104 = (s32[32,128]{1,0:T(8,128)}, s32[1,2048]{1,0:T(1,128)}) custom-call(s32[1,2048]{1,0:T(1,128)} %bitcast.3, s32[1,2048]{1,0:T(1,128)} %bitcast.2), custom_call_target="tpu_custom_call" | custom-call | tf_op jit(solution)/shard_map/pallas_call | solution.py:60
  3.6 83.3 %shard_map.105 = (f32[128,32,128]{2,1,0:T(8,128)}, f32[8192,128]{1,0:T(8,128)}) custom-call(s32[32,128]{1,0:T(8,128)} %get-tuple-element.7.pick_ref, f32[64,64,128]{2,1,0:T(8,128)} %u_hbm.1, f32[64,64,128]{2,1,0:T(8,128)} %v_hbm.1, f32[64,128]{1,0:T(8,128)} %d_hbm.1, f32[1,128,256]{2,1,0:T(8,128)} %w1_hbm.1, f32[1,256,256]{2,1,0:T(8,128)} %w2_hbm.1, ...), custom_call_target="tpu_custom_call" | custom-call | tf_op jit(solution)/shard_map/pallas_call | solution.py:474
  86.9 10.2 %shard_map.106 = (f32[64,64,128]{2,1,0:T(8,128)}, f32[64,64,128]{2,1,0:T(8,128)}) custom-call(s32[2048]{0:T(1024)} %column_ref.1, s32[1,2048]{1,0:T(1,128)} %get-tuple-element.6.slot_ref, f32[128,32,128]{2,1,0:T(8,128)} %get-tuple-element.8.drag_ref, f32[8192,128]{1,0:T(8,128)} %get-tuple-element.9.diffused_hbm), custom_call_target="tpu_custom_call" | custom-call | tf_op jit(solution)/shard_map/pallas_call | solution.py:567

commit v4 on v3

--- a/solution.py
+++ b/solution.py
@@ -22,10 +22,11 @@
 ROWS_X = WX + 8
 ROWS_Y = WY + 32
 GROUP = 16
+PADDED = WX + 8
 GROUPS = DEVICES // GROUP
 
 
-def slot_kernel(regime_ref, column_ref, pick_ref, slot_ref):
+def find_slots(regime_ref, column_ref, pick_ref, slot_ref):
     width = 256
     blocks = ACTIVE // width
     expert = lax.broadcasted_iota(jnp.int32, (DEVICES, width), 0)
@@ -52,20 +53,7 @@
         dims = (((1,), (1,)), ((), ()))
         pick_x = pick_x + lax.dot_general((chosen * x).astype(BF16), hit16, dims, preferred_element_type=F32)
         pick_y = pick_y + lax.dot_general((chosen * y).astype(BF16), hit16, dims, preferred_element_type=F32)
-    pick_ref[...] = (pick_x * WY + pick_y).astype(jnp.int32)
-
-
-def find_slots(regimes, active_columns):
-    vmem = pl.BlockSpec(memory_space=pltpu.VMEM)
-    return pl.pallas_call(
-        slot_kernel,
-        out_shape=(
-            jax.ShapeDtypeStruct((CAP, DEVICES), jnp.int32),
-            jax.ShapeDtypeStruct((1, ACTIVE), jnp.int32),
-        ),
-        in_specs=[vmem, vmem],
-        out_specs=(vmem, vmem),
-    )(regimes.reshape(1, ACTIVE), active_columns.reshape(1, ACTIVE))
+    pick_ref[...] = jnp.clip((pick_x * WY + pick_y).astype(jnp.int32), 0, WX * WY - 1)
 
 
 NEIGHBOURS = [(dx, dy) for dx in (-1, 0, 1) for dy in (-1, 0, 1) if (dx, dy) != (0, 0)]
@@ -89,7 +77,8 @@
 
 
 def main_kernel(
-    pick_ref,
+    regime_ref,
+    column_ref,
     u_hbm,
     v_hbm,
     d_hbm,
@@ -99,6 +88,9 @@
     w4_hbm,
     drag_ref,
     diffused_hbm,
+    slot_ref,
+    pick_vmem,
+    pick_ref,
     fields,
     profiles,
     state,
@@ -132,6 +124,7 @@
     back_send,
     back_recv,
     diffused_sem,
+    pick_sem,
 ):
     tile = lax.axis_index("tile")
     inf = lax.axis_index("inf")
@@ -161,30 +154,26 @@
 
     barrier = pltpu.get_barrier_semaphore()
 
-    def greet(step):
+    def greet(step, carry):
         other = me + step
         other = jnp.where(other >= DEVICES, other - DEVICES, other)
         pl.semaphore_signal(barrier, inc=1, device_id=other, device_id_type=LOGICAL)
-
-    flat_fields = fields.reshape(2 * LEVELS * WX, WY)
+        return carry
+
+    lax.fori_loop(1, DEVICES, greet, 0)
+
+    find_slots(regime_ref, column_ref, pick_vmem, slot_ref)
+    picks = pltpu.make_async_copy(pick_vmem, pick_ref, pick_sem)
+    picks.start()
+
+    flat_fields = fields.reshape(2 * LEVELS * PADDED, WY)
 
     def turn(step, carry):
         for k in range(4):
             x = 4 * step + k
-            if k < 3:
-                greet(2 * x + 1)
-                greet(2 * x + 2)
-            block = flat_fields[pl.ds(x, FEATURES, stride=WX), :].T
+            block = flat_fields[pl.ds(x, FEATURES, stride=PADDED), :].T
             state[0, x + 4, 16 : 16 + WY, :] = block
             profiles[pl.ds(pl.multiple_of(x * WY, WY), WY), :] = block
-        x = 4 * step + 3
-
-        greet(2 * x + 1)
-
-        @pl.when(step < WX // 4 - 1)
-        def _():
-            greet(2 * x + 2)
-
         return carry
 
     for piece in range(pieces):
@@ -192,6 +181,7 @@
         loads[2 * piece + 1].wait()
         lax.fori_loop(piece * wide // 4, (piece + 1) * wide // 4, turn, 0)
     own_d.wait()
+    picks.wait()
 
     @pl.when(tile == 0)
     def _():
@@ -418,27 +408,14 @@
 
         network(group, carry)
 
-        @pl.when(group == 1)
-        def _():
-            receive_halo()
-            lax.fori_loop(0, ROWS_X // 8, widen, 0)
-
-        @pl.when(group == 3)
-        def _():
-            lax.fori_loop(ROWS_X // 8, ROWS_X // 4, widen, 0)
-
-        @pl.when(group == 4)
-        def _():
-            diffuse(0)
-
-        @pl.when(group == 5)
-        def _():
-            diffuse(1)
-
         return carry
 
     lax.fori_loop(0, GROUPS, arrived_network, 0)
     drag_ref[me] = answer[0]
+    receive_halo()
+    lax.fori_loop(0, ROWS_X // 4, widen, 0)
+    diffuse(0)
+    diffuse(1)
     diffuse(2)
     diffuse(3)
     diffused = pltpu.make_async_copy(profiles, diffused_hbm, diffused_sem)
@@ -464,9 +441,8 @@
     diffused.wait()
 
 
-def drag_and_diffusion(pick, u_field, v_field, diffusivity, layers):
+def drag_and_diffusion(regimes, active_columns, u_field, v_field, diffusivity, layers):
     vmem = pl.BlockSpec(memory_space=pltpu.VMEM)
-    smem = pl.BlockSpec(memory_space=pltpu.SMEM)
     hbm = pl.BlockSpec(memory_space=pltpu.HBM)
     shapes = [layer.shape[1:] for layer in layers]
     halves = [pltpu.VMEM(shape, BF16) for shape in shapes for _ in range(2)]
@@ -476,11 +452,14 @@
         out_shape=(
             jax.ShapeDtypeStruct((DEVICES, CAP, FEATURES), F32),
             jax.ShapeDtypeStruct((WX * WY, FEATURES), F32),
+            jax.ShapeDtypeStruct((1, ACTIVE), jnp.int32),
         ),
-        in_specs=[smem] + [hbm] * 7,
-        out_specs=(vmem, hbm),
+        in_specs=[vmem, vmem] + [hbm] * 7,
+        out_specs=(vmem, hbm, vmem),
         scratch_shapes=[
-            pltpu.VMEM((2, LEVELS, WX, WY), F32),
+            pltpu.VMEM((CAP, DEVICES), jnp.int32),
+            pltpu.SMEM((CAP, DEVICES), jnp.int32),
+            pltpu.VMEM((2, LEVELS, PADDED, WY), F32),
             pltpu.VMEM((WX * WY, FEATURES), F32),
             pltpu.VMEM((2, ROWS_X, ROWS_Y, FEATURES), F32),
             pltpu.VMEM((3, WX + 16, WY), F32),
@@ -503,11 +482,12 @@
             dma,
             dma,
             dma,
+            dma,
         ],
         compiler_params=pltpu.CompilerParams(
             collective_id=0, has_side_effects=True, vmem_limit_bytes=59840 << 10
         ),
-    )(pick, u_field, v_field, diffusivity, *layers)
+    )(regimes.reshape(1, ACTIVE), active_columns.reshape(1, ACTIVE), u_field, v_field, diffusivity, *layers)
 
 
 def place_kernel(
@@ -536,14 +516,14 @@
         return carry
 
     lax.fori_loop(0, ACTIVE // 16, place, 0)
-    flat = staged.reshape(2 * LEVELS * WX, WY)
+    flat = staged.reshape(2 * LEVELS * PADDED, WY)
 
     def turn(step, carry):
         for k in range(4):
             x = 4 * step + k
             part = pl.ds(pl.multiple_of(x * WY, WY), WY)
             block = dense[part, :] + diffused[part, :]
-            flat[pl.ds(x, FEATURES, stride=WX), :] = block.T
+            flat[pl.ds(x, FEATURES, stride=PADDED), :] = block.T
         return carry
 
     copies = []
@@ -572,7 +552,7 @@
         scratch_shapes=[
             pltpu.VMEM((WX * WY, FEATURES), F32),
             pltpu.VMEM((WX * WY, FEATURES), F32),
-            pltpu.VMEM((2, LEVELS, WX, WY), F32),
+            pltpu.VMEM((2, LEVELS, PADDED, WY), F32),
             pltpu.SemaphoreType.DMA((4,)),
             pltpu.SemaphoreType.DMA((4, 2)),
         ],
@@ -591,9 +571,8 @@
     third_layer,
     last_layer,
 ):
-    pick, slots = find_slots(regimes, active_columns)
     layers = (first_layer, second_layer, third_layer, last_layer)
-    drag, diffused = drag_and_diffusion(pick, u_field, v_field, diffusivity, layers)
+    drag, diffused, slots = drag_and_diffusion(regimes, active_columns, u_field, v_field, diffusivity, layers)
     return place_drag(active_columns, slots, drag, diffused)
 
 

time: 97.5 us -> 86.8 us (0.89)
  Pallas kernels: 96.4 us -> 85.9 us
    pallas_call x1, Pallas kernels: 83.3 us -> 77.5 us  [drag_and_diffusion(): pl.pallas_call(main_kernel, out_shape=(jax.ShapeDtypeStruct((DEVICES, CAP...]
    pallas_call x1 -> x0, Pallas kernels: 2.97 us -> none  [find_slots(): pl.pallas_call(slot_kernel, out_shape=(jax.ShapeDtypeStruct((CAP, DEVICES...]
    pallas_call x1, Pallas kernels: 10.2 us -> 8.41 us  [place_drag(): pl.pallas_call(place_kernel, out_shape=(shape, shape), in_specs=[smem, sm...]
where the time goes in v4:
time: 86.8 us; the launch traced here: 86.6 us
  Pallas kernels  85.9 us (99%)
    pallas_call x1, Pallas kernels, drag_and_diffusion(): pl.pallas_call(main_kernel, out_shape=(jax.ShapeDtypeStruct((DEVICES, CAP...  77.5 us
    pallas_call x1, Pallas kernels, place_drag(): pl.pallas_call(place_kernel, out_shape=(shape, shape), in_specs=[smem, sm...  8.41 us

profile of v4, /device:TPU:1, one launch (start us, length us, event | category | flops | bytes accessed | tf_op | source)
XLA Modules:
  0.0 86.6 jit_solution(5615595061611362798)
XLA Ops:
  0.6 77.5 %shard_map.104 = (f32[128,32,128]{2,1,0:T(8,128)}, f32[8192,128]{1,0:T(8,128)}, s32[1,2048]{1,0:T(1,128)}) custom-call(s32[1,2048]{1,0:T(1,128)} %bitcast.3, s32[1,2048]{1,0:T(1,128)} %bitcast.2, f32[64,64,128]{2,1,0:T(8,128)} %u_hbm.1, f32[64,64,128]{2,1,0:T(8,128)} %v_hbm.1, f32[64,128]{1,0:T(8,128)} %d_hbm.1, f32[1,128,256]{2,1,0:T(8,128)} %w1_hbm.1, ...), custom_call_target="tpu_custom_call" | custom-call | tf_op jit(solution)/shard_map/pallas_call | solution.py:450
  78.2 8.4 %shard_map.105 = (f32[64,64,128]{2,1,0:T(8,128)}, f32[64,64,128]{2,1,0:T(8,128)}) custom-call(s32[2048]{0:T(1024)} %column_ref.1, s32[1,2048]{1,0:T(1,128)} %get-tuple-element.5.slot_ref, f32[128,32,128]{2,1,0:T(8,128)} %get-tuple-element.6.drag_ref, f32[8192,128]{1,0:T(8,128)} %get-tuple-element.7.diffused_hbm), custom_call_target="tpu_custom_call" | custom-call | tf_op jit(solution)/shard_map/pallas_call | solution.py:547

commit v5 on v4

--- a/solution.py
+++ b/solution.py
@@ -21,9 +21,10 @@
 ACTIVE = 2048
 ROWS_X = WX + 8
 ROWS_Y = WY + 32
-GROUP = 16
+GROUP = 32
 PADDED = WX + 8
 GROUPS = DEVICES // GROUP
+TURNS = GROUP // 8
 
 
 def find_slots(regime_ref, column_ref, pick_ref, slot_ref):
@@ -86,7 +87,7 @@
     w2_hbm,
     w3_hbm,
     w4_hbm,
-    drag_ref,
+    drag_hbm,
     diffused_hbm,
     slot_ref,
     pick_vmem,
@@ -272,7 +273,7 @@
     def back(step, other):
         return pltpu.make_async_remote_copy(
             src_ref=answer.at[step],
-            dst_ref=drag_ref.at[me],
+            dst_ref=drag_hbm.at[me],
             send_sem=back_send,
             recv_sem=back_recv,
             device_id=other,
@@ -290,9 +291,9 @@
 
                 @pl.when(turn_number > 0)
                 def _():
-                    away(step, other, turn_number // 2).start()
+                    away(step, other, turn_number // TURNS).start()
             else:
-                away(step, other, turn_number // 2).start()
+                away(step, other, turn_number // TURNS).start()
         return carry
 
     lax.fori_loop(0, DEVICES // 8, dispatch, 0)
@@ -373,9 +374,9 @@
         hidden = silu(product(hidden, w3h, w3l))
         result = product(hidden, w4h, w4l)
         answer[pl.ds(group * GROUP, GROUP)] = result.reshape(GROUP, CAP, FEATURES)
-        for part in range(2):
+        for part in range(TURNS):
             for lane in range(8):
-                turn_number = group * 2 + part
+                turn_number = group * TURNS + part
                 step = turn_number * 8 + lane
                 other = source(turn_number, lane)
                 if part == 0 and lane == 0:
@@ -411,7 +412,8 @@
         return carry
 
     lax.fori_loop(0, GROUPS, arrived_network, 0)
-    drag_ref[me] = answer[0]
+    own_answer = pltpu.make_async_copy(answer.at[0], drag_hbm.at[me], own_sem)
+    own_answer.start()
     receive_halo()
     lax.fori_loop(0, ROWS_X // 4, widen, 0)
     diffuse(0)
@@ -424,7 +426,7 @@
     others = DEVICES - 1
     pltpu.make_async_remote_copy(
         src_ref=answer.at[pl.ds(0, others)],
-        dst_ref=drag_ref.at[pl.ds(0, others)],
+        dst_ref=drag_hbm.at[pl.ds(0, others)],
         send_sem=back_send,
         recv_sem=back_recv,
         device_id=me,
@@ -439,6 +441,7 @@
         device_id_type=LOGICAL,
     ).wait_send()
     diffused.wait()
+    own_answer.wait()
 
 
 def drag_and_diffusion(regimes, active_columns, u_field, v_field, diffusivity, layers):
@@ -455,7 +458,7 @@
             jax.ShapeDtypeStruct((1, ACTIVE), jnp.int32),
         ),
         in_specs=[vmem, vmem] + [hbm] * 7,
-        out_specs=(vmem, hbm, vmem),
+        out_specs=(hbm, hbm, vmem),
         scratch_shapes=[
             pltpu.VMEM((CAP, DEVICES), jnp.int32),
             pltpu.SMEM((CAP, DEVICES), jnp.int32),
@@ -491,15 +494,16 @@
 
 
 def place_kernel(
-    column_ref, slot_ref, drag_ref, diffused_hbm, u_hbm, v_hbm, dense, diffused, staged, in_sem, out_sem
+    column_ref, slot_ref, drag_hbm, diffused_hbm, u_hbm, v_hbm, drag, dense, diffused, staged, drag_sem, in_sem, out_sem
 ):
     pieces = 4
     wide = WX // pieces
+    drag_load = pltpu.make_async_copy(drag_hbm, drag, drag_sem)
+    drag_load.start()
     loads = []
     for piece in range(pieces):
         part = pl.ds(piece * wide * WY, wide * WY)
         load = pltpu.make_async_copy(diffused_hbm.at[part], diffused.at[part], in_sem.at[piece])
-        load.start()
         loads.append(load)
 
     def clear(x, carry):
@@ -507,20 +511,23 @@
         return carry
 
     lax.fori_loop(0, WX, clear, 0)
-    drags = drag_ref.reshape(DEVICES * CAP, FEATURES)
+    drag_load.wait()
+    for load in loads:
+        load.start()
+    drags = drag.reshape(DEVICES * CAP, FEATURES)
 
     def place(step, carry):
-        rows = [drags[pl.ds(slot_ref[0, step * 16 + k], 1), :] for k in range(16)]
-        for k in range(16):
-            dense[pl.ds(column_ref[step * 16 + k], 1), :] = rows[k]
-        return carry
-
-    lax.fori_loop(0, ACTIVE // 16, place, 0)
+        rows = [drags[pl.ds(slot_ref[0, step * 32 + k], 1), :] for k in range(32)]
+        for k in range(32):
+            dense[pl.ds(column_ref[step * 32 + k], 1), :] = rows[k]
+        return carry
+
+    lax.fori_loop(0, ACTIVE // 32, place, 0)
     flat = staged.reshape(2 * LEVELS * PADDED, WY)
 
     def turn(step, carry):
-        for k in range(4):
-            x = 4 * step + k
+        for k in range(8):
+            x = 8 * step + k
             part = pl.ds(pl.multiple_of(x * WY, WY), WY)
             block = dense[part, :] + diffused[part, :]
             flat[pl.ds(x, FEATURES, stride=PADDED), :] = block.T
@@ -529,7 +536,7 @@
     copies = []
     for piece in range(pieces):
         loads[piece].wait()
-        lax.fori_loop(piece * wide // 4, (piece + 1) * wide // 4, turn, 0)
+        lax.fori_loop(piece * wide // 8, (piece + 1) * wide // 8, turn, 0)
         part = pl.ds(piece * wide, wide)
         for which, target in enumerate((u_hbm, v_hbm)):
             copy = pltpu.make_async_copy(staged.at[which, :, part, :], target.at[:, part, :], out_sem.at[piece, which])
@@ -540,19 +547,20 @@
 
 
 def place_drag(active_columns, slots, drag, diffused):
-    vmem = pl.BlockSpec(memory_space=pltpu.VMEM)
     smem = pl.BlockSpec(memory_space=pltpu.SMEM)
     hbm = pl.BlockSpec(memory_space=pltpu.HBM)
     shape = jax.ShapeDtypeStruct((LEVELS, WX, WY), F32)
     return pl.pallas_call(
         place_kernel,
         out_shape=(shape, shape),
-        in_specs=[smem, smem, vmem, hbm],
+        in_specs=[smem, smem, hbm, hbm],
         out_specs=(hbm, hbm),
         scratch_shapes=[
+            pltpu.VMEM((DEVICES, CAP, FEATURES), F32),
             pltpu.VMEM((WX * WY, FEATURES), F32),
             pltpu.VMEM((WX * WY, FEATURES), F32),
             pltpu.VMEM((2, LEVELS, PADDED, WY), F32),
+            pltpu.SemaphoreType.DMA,
             pltpu.SemaphoreType.DMA((4,)),
             pltpu.SemaphoreType.DMA((4, 2)),
         ],

time: 86.8 us -> 84.2 us (0.970)
  Pallas kernels: 85.9 us -> 83.3 us
    pallas_call x1, Pallas kernels: 77.5 us -> 75.1 us  [drag_and_diffusion(): pl.pallas_call(main_kernel, out_shape=(jax.ShapeDtypeStruct((DEVICES, CAP...]
where the time goes in v5:
time: 84.2 us; the launch traced here: 83.9 us
  Pallas kernels  83.3 us (99%)
    pallas_call x1, Pallas kernels, drag_and_diffusion(): pl.pallas_call(main_kernel, out_shape=(jax.ShapeDtypeStruct((DEVICES, CAP...  75.1 us
    pallas_call x1, Pallas kernels, place_drag(): pl.pallas_call(place_kernel, out_shape=(shape, shape), in_specs=[smem, sm...  8.14 us

profile of v5, /device:TPU:1, one launch (start us, length us, event | category | flops | bytes accessed | tf_op | source)
XLA Modules:
  0.0 83.9 jit_solution(1780126790728011001)
XLA Ops:
  0.6 75.1 %shard_map.104 = (f32[128,32,128]{2,1,0:T(8,128)}, f32[8192,128]{1,0:T(8,128)}, s32[1,2048]{1,0:T(1,128)}) custom-call(s32[1,2048]{1,0:T(1,128)} %bitcast.3, s32[1,2048]{1,0:T(1,128)} %bitcast.2, f32[64,64,128]{2,1,0:T(8,128)} %u_hbm.1, f32[64,64,128]{2,1,0:T(8,128)} %v_hbm.1, f32[64,128]{1,0:T(8,128)} %d_hbm.1, f32[1,128,256]{2,1,0:T(8,128)} %w1_hbm.1, ...), custom_call_target="tpu_custom_call" | custom-call | tf_op jit(solution)/shard_map/pallas_call | solution.py:453
  75.8 8.1 %shard_map.105 = (f32[64,64,128]{2,1,0:T(8,128)}, f32[64,64,128]{2,1,0:T(8,128)}) custom-call(s32[2048]{0:T(1024)} %column_ref.1, s32[1,2048]{1,0:T(1,128)} %get-tuple-element.5.slot_ref, f32[128,32,128]{2,1,0:T(8,128)} %get-tuple-element.6.drag_hbm, f32[8192,128]{1,0:T(8,128)} %get-tuple-element.7.diffused_hbm), custom_call_target="tpu_custom_call" | custom-call | tf_op jit(solution)/shard_map/pallas_call | solution.py:553

commit v6 on v5

--- a/solution.py
+++ b/solution.py
@@ -25,6 +25,7 @@
 PADDED = WX + 8
 GROUPS = DEVICES // GROUP
 TURNS = GROUP // 8
+AHEAD = 3
 
 
 def find_slots(regime_ref, column_ref, pick_ref, slot_ref):
@@ -296,7 +297,7 @@
                 away(step, other, turn_number // TURNS).start()
         return carry
 
-    lax.fori_loop(0, DEVICES // 8, dispatch, 0)
+    lax.fori_loop(0, AHEAD * TURNS, dispatch, 0)
     recv[0] = send[0]
 
     for load in weight_loads:
@@ -406,6 +407,11 @@
         @pl.when(group > 0)
         def _():
             arrived(group * GROUP, GROUP, group)
+
+        @pl.when(group < GROUPS - AHEAD)
+        def _():
+            first = (group + AHEAD) * TURNS
+            lax.fori_loop(first, first + TURNS, dispatch, 0)
 
         network(group, carry)
 

time: 84.2 us -> 82.6 us (0.981)
  Pallas kernels: 83.3 us -> 81.6 us
    pallas_call x1, Pallas kernels: 75.1 us -> 73.5 us  [drag_and_diffusion(): pl.pallas_call(main_kernel, out_shape=(jax.ShapeDtypeStruct((DEVICES, CAP...]
where the time goes in v6:
time: 82.6 us; the launch traced here: 82.3 us
  Pallas kernels  81.6 us (99%)
    pallas_call x1, Pallas kernels, drag_and_diffusion(): pl.pallas_call(main_kernel, out_shape=(jax.ShapeDtypeStruct((DEVICES, CAP...  73.5 us
    pallas_call x1, Pallas kernels, place_drag(): pl.pallas_call(place_kernel, out_shape=(shape, shape), in_specs=[smem, sm...  8.14 us

profile of v6, /device:TPU:1, one launch (start us, length us, event | category | flops | bytes accessed | tf_op | source)
XLA Modules:
  0.0 82.3 jit_solution(11462025303262087266)
XLA Ops:
  0.6 73.5 %shard_map.104 = (f32[128,32,128]{2,1,0:T(8,128)}, f32[8192,128]{1,0:T(8,128)}, s32[1,2048]{1,0:T(1,128)}) custom-call(s32[1,2048]{1,0:T(1,128)} %bitcast.3, s32[1,2048]{1,0:T(1,128)} %bitcast.2, f32[64,64,128]{2,1,0:T(8,128)} %u_hbm.1, f32[64,64,128]{2,1,0:T(8,128)} %v_hbm.1, f32[64,128]{1,0:T(8,128)} %d_hbm.1, f32[1,128,256]{2,1,0:T(8,128)} %w1_hbm.1, ...), custom_call_target="tpu_custom_call" | custom-call | tf_op jit(solution)/shard_map/pallas_call | solution.py:459
  74.1 8.1 %shard_map.105 = (f32[64,64,128]{2,1,0:T(8,128)}, f32[64,64,128]{2,1,0:T(8,128)}) custom-call(s32[2048]{0:T(1024)} %column_ref.1, s32[1,2048]{1,0:T(1,128)} %get-tuple-element.5.slot_ref, f32[128,32,128]{2,1,0:T(8,128)} %get-tuple-element.6.drag_hbm, f32[8192,128]{1,0:T(8,128)} %get-tuple-element.7.diffused_hbm), custom_call_target="tpu_custom_call" | custom-call | tf_op jit(solution)/shard_map/pallas_call | solution.py:559

commit v7 on v6

--- a/solution.py
+++ b/solution.py
@@ -415,13 +415,17 @@
 
         network(group, carry)
 
+        @pl.when(group == GROUPS - 2)
+        def _():
+            receive_halo()
+            lax.fori_loop(0, ROWS_X // 4, widen, 0)
+
+
         return carry
 
     lax.fori_loop(0, GROUPS, arrived_network, 0)
     own_answer = pltpu.make_async_copy(answer.at[0], drag_hbm.at[me], own_sem)
     own_answer.start()
-    receive_halo()
-    lax.fori_loop(0, ROWS_X // 4, widen, 0)
     diffuse(0)
     diffuse(1)
     diffuse(2)

time: 82.6 us -> 82.6 us (level)
  no operation moved by 1% of the time
where the time goes in v7:
time: 82.6 us; the launch traced here: 82.3 us
  Pallas kernels  81.6 us (99%)
    pallas_call x1, Pallas kernels, drag_and_diffusion(): pl.pallas_call(main_kernel, out_shape=(jax.ShapeDtypeStruct((DEVICES, CAP...  73.5 us
    pallas_call x1, Pallas kernels, place_drag(): pl.pallas_call(place_kernel, out_shape=(shape, shape), in_specs=[smem, sm...  8.14 us

profile of v7, /device:TPU:1, one launch (start us, length us, event | category | flops | bytes accessed | tf_op | source)
XLA Modules:
  0.0 82.3 jit_solution(9602092286487494371)
XLA Ops:
  0.6 73.5 %shard_map.104 = (f32[128,32,128]{2,1,0:T(8,128)}, f32[8192,128]{1,0:T(8,128)}, s32[1,2048]{1,0:T(1,128)}) custom-call(s32[1,2048]{1,0:T(1,128)} %bitcast.3, s32[1,2048]{1,0:T(1,128)} %bitcast.2, f32[64,64,128]{2,1,0:T(8,128)} %u_hbm.1, f32[64,64,128]{2,1,0:T(8,128)} %v_hbm.1, f32[64,128]{1,0:T(8,128)} %d_hbm.1, f32[1,128,256]{2,1,0:T(8,128)} %w1_hbm.1, ...), custom_call_target="tpu_custom_call" | custom-call | tf_op jit(solution)/shard_map/pallas_call | solution.py:463
  74.1 8.1 %shard_map.105 = (f32[64,64,128]{2,1,0:T(8,128)}, f32[64,64,128]{2,1,0:T(8,128)}) custom-call(s32[2048]{0:T(1024)} %column_ref.1, s32[1,2048]{1,0:T(1,128)} %get-tuple-element.5.slot_ref, f32[128,32,128]{2,1,0:T(8,128)} %get-tuple-element.6.drag_hbm, f32[8192,128]{1,0:T(8,128)} %get-tuple-element.7.diffused_hbm), custom_call_target="tpu_custom_call" | custom-call | tf_op jit(solution)/shard_map/pallas_call | solution.py:563
